TPU v7x, 32 devices: a whole 2x2x4 slice. The times are simulated.
32 devices in a mesh: dp: 4 (over y, x), side: 2 (over core), seq: 4 (over z).
Axes of the slice: x: 2, y: 2, z: 4, core: 2. Of those that a mesh axis runs over, the one named last changes fastest.
Arguments:
- tokens: bfloat16 [8192, 768], P(('dp', 'side', 'seq')), may hold values from -6 to 6
- head_in: bfloat16 [8192, 1024], P(('dp', 'side', 'seq')), may hold values from -6 to 6
- image_ids: int32 [8192], P(('dp', 'side', 'seq')), may hold values from 0 to 1, as said below
- out_cotangent: bfloat16 [8192, 768], P(('dp', 'side', 'seq')), may hold values from -6 to 6
- head_cotangent: bfloat16 [8192, 1024], P(('dp', 'side', 'seq')), may hold values from -6 to 6
- weight_attend: float32 [768, 2304], P(('dp', 'side', 'seq')), may hold values from -0.21875 to 0.21875
- weight_proj: float32 [768, 768], P(('dp', 'side', 'seq')), may hold values from -1.75 to 1.75
- weight_up: float32 [768, 3072], P(('dp', 'side', 'seq')), may hold values from -0.21875 to 0.21875
- weight_down: float32 [3072, 768], P(('dp', 'side', 'seq')), may hold values from -0.109375 to 0.109375
- weight_cond: float32 [768, 1024], P(('dp', 'side', 'seq')), may hold values from -0.21875 to 0.21875
- weight_mod: float32 [1024, 3072], P(('dp', 'side', 'seq')), may hold values from -0.1875 to 0.1875
- weight_inner: float32 [1024, 1024], P(('dp', 'side', 'seq')), may hold values from -0.1875 to 0.1875
- weight_outer: float32 [1024, 1024], P(('dp', 'side', 'seq')), may hold values from -0.1875 to 0.1875
- norm_params: float32 [768, 4], P(('dp', 'side', 'seq')), as said below
- mean_attend: float32 [768, 2304], P(('dp', 'side', 'seq')), may hold values from -0.375 to 0.375
- mean_proj: float32 [768, 768], P(('dp', 'side', 'seq')), may hold values from -0.375 to 0.375
- mean_up: float32 [768, 3072], P(('dp', 'side', 'seq')), may hold values from -0.375 to 0.375
- mean_down: float32 [3072, 768], P(('dp', 'side', 'seq')), may hold values from -0.375 to 0.375
- mean_cond: float32 [768, 1024], P(('dp', 'side', 'seq')), may hold values from -0.375 to 0.375
- mean_mod: float32 [1024, 3072], P(('dp', 'side', 'seq')), may hold values from -0.375 to 0.375
- mean_inner: float32 [1024, 1024], P(('dp', 'side', 'seq')), may hold values from -0.375 to 0.375
- mean_outer: float32 [1024, 1024], P(('dp', 'side', 'seq')), may hold values from -0.375 to 0.375
- mean_norms: float32 [768, 4], P(('dp', 'side', 'seq')), may hold values from -0.375 to 0.375
- square_attend: float32 [768, 2304], P(('dp', 'side', 'seq')), may hold values from 0.0085 to 0.135
- square_proj: float32 [768, 768], P(('dp', 'side', 'seq')), may hold values from 0.0021 to 0.034
- square_up: float32 [768, 3072], P(('dp', 'side', 'seq')), may hold values from 0.0085 to 0.135
- square_down: float32 [3072, 768], P(('dp', 'side', 'seq')), may hold values from 0.0085 to 0.135
- square_cond: float32 [768, 1024], P(('dp', 'side', 'seq')), may hold values from 0.0085 to 0.135
- square_mod: float32 [1024, 3072], P(('dp', 'side', 'seq')), may hold values from 0.0085 to 0.135
- square_inner: float32 [1024, 1024], P(('dp', 'side', 'seq')), may hold values from 0.0085 to 0.135
- square_outer: float32 [1024, 1024], P(('dp', 'side', 'seq')), may hold values from 0.0085 to 0.135
- square_norms: float32 [768, 4], P(('dp', 'side', 'seq')), may hold values from 0.0085 to 0.135
- ema_attend: float32 [768, 2304], P(('dp', 'side', 'seq')), may hold values from -0.21875 to 0.21875
- ema_proj: float32 [768, 768], P(('dp', 'side', 'seq')), may hold values from -1.75 to 1.75
- ema_up: float32 [768, 3072], P(('dp', 'side', 'seq')), may hold values from -0.21875 to 0.21875
- ema_down: float32 [3072, 768], P(('dp', 'side', 'seq')), may hold values from -0.109375 to 0.109375
- ema_cond: float32 [768, 1024], P(('dp', 'side', 'seq')), may hold values from -0.21875 to 0.21875
- ema_mod: float32 [1024, 3072], P(('dp', 'side', 'seq')), may hold values from -0.1875 to 0.1875
- ema_inner: float32 [1024, 1024], P(('dp', 'side', 'seq')), may hold values from -0.1875 to 0.1875
- ema_outer: float32 [1024, 1024], P(('dp', 'side', 'seq')), may hold values from -0.1875 to 0.1875
- ema_norms: float32 [768, 4], P(('dp', 'side', 'seq')), may hold values from -1 to 1.5
Outputs:
- block_out: bfloat16 [8192, 768], P(('dp', 'side', 'seq'))
- head_out: bfloat16 [8192, 1024], P(('dp', 'side', 'seq'))
- tokens_grad: float32 [8192, 768], P(('dp', 'side', 'seq'))
- head_in_grad: float32 [8192, 1024], P(('dp', 'side', 'seq'))
- grad_norm: float32 [], replicated
- new_attend: float32 [768, 2304], P(('dp', 'side', 'seq'))
- new_mean_attend: float32 [768, 2304], P(('dp', 'side', 'seq'))
- new_square_attend: float32 [768, 2304], P(('dp', 'side', 'seq'))
- new_proj: float32 [768, 768], P(('dp', 'side', 'seq'))
- new_mean_proj: float32 [768, 768], P(('dp', 'side', 'seq'))
- new_square_proj: float32 [768, 768], P(('dp', 'side', 'seq'))
- new_up: float32 [768, 3072], P(('dp', 'side', 'seq'))
- new_mean_up: float32 [768, 3072], P(('dp', 'side', 'seq'))
- new_square_up: float32 [768, 3072], P(('dp', 'side', 'seq'))
- new_down: float32 [3072, 768], P(('dp', 'side', 'seq'))
- new_mean_down: float32 [3072, 768], P(('dp', 'side', 'seq'))
- new_square_down: float32 [3072, 768], P(('dp', 'side', 'seq'))
- new_cond: float32 [768, 1024], P(('dp', 'side', 'seq'))
- new_mean_cond: float32 [768, 1024], P(('dp', 'side', 'seq'))
- new_square_cond: float32 [768, 1024], P(('dp', 'side', 'seq'))
- new_mod: float32 [1024, 3072], P(('dp', 'side', 'seq'))
- new_mean_mod: float32 [1024, 3072], P(('dp', 'side', 'seq'))
- new_square_mod: float32 [1024, 3072], P(('dp', 'side', 'seq'))
- new_inner: float32 [1024, 1024], P(('dp', 'side', 'seq'))
- new_mean_inner: float32 [1024, 1024], P(('dp', 'side', 'seq'))
- new_square_inner: float32 [1024, 1024], P(('dp', 'side', 'seq'))
- new_outer: float32 [1024, 1024], P(('dp', 'side', 'seq'))
- new_mean_outer: float32 [1024, 1024], P(('dp', 'side', 'seq'))
- new_square_outer: float32 [1024, 1024], P(('dp', 'side', 'seq'))
- new_norms: float32 [768, 4], P(('dp', 'side', 'seq'))
- new_mean_norms: float32 [768, 4], P(('dp', 'side', 'seq'))
- new_square_norms: float32 [768, 4], P(('dp', 'side', 'seq'))
- new_ema_attend: float32 [768, 2304], P(('dp', 'side', 'seq'))
- new_ema_proj: float32 [768, 768], P(('dp', 'side', 'seq'))
- new_ema_up: float32 [768, 3072], P(('dp', 'side', 'seq'))
- new_ema_down: float32 [3072, 768], P(('dp', 'side', 'seq'))
- new_ema_cond: float32 [768, 1024], P(('dp', 'side', 'seq'))
- new_ema_mod: float32 [1024, 3072], P(('dp', 'side', 'seq'))
- new_ema_inner: float32 [1024, 1024], P(('dp', 'side', 'seq'))
- new_ema_outer: float32 [1024, 1024], P(('dp', 'side', 'seq'))
- new_ema_norms: float32 [768, 4], P(('dp', 'side', 'seq'))
Inputs may be any that keep to these rules, and one draw needn't show every extreme that they name: `image_ids`: within each device's block of 256 tokens the image numbers never fall; the visible and the masked block of a pair use the same numbers, with uneven counts. `norm_params`: columns 0 and 2 are gains between 0.2 and 1.8, columns 1 and 3 biases.
All inputs are finite; a program needn't handle non-finite values.
Results may differ from a plain program's by a relative error of at most 0.025.
Values may be sent and summed in bfloat16 or wider, within the bound.
A program may use at most 192 MiB of HBM per device.

v0:
```python
import jax
import jax.numpy as jnp
from jax import lax
from jax.sharding import PartitionSpec as P

D = 768
HEADS = 12
HEAD_DIM = 64
HW = 1024
STEP = 5


norm_eps = 1e-06
clip_limit = 2048.0
learn_rates = (0.03, 0.24, 0.03, 0.03, 0.03, 0.03, 0.03, 0.03, 0.4)
beta_first = 0.9
beta_second = 0.95
weight_decay = 0.02
adam_eps = 1e-08
ema_decay = 0.9999
masked_fill = -1e30


def shifted(value, axis, steps):
    count = lax.axis_size(axis)
    first, last = (max(0, -steps), min(count, count - steps))
    return lax.ppermute(value, axis, [(source, source + steps) for source in range(first, last)])


def layer_norm(values):
    centre = values - jnp.mean(values, axis=-1, keepdims=True)
    spread = jnp.mean(centre * centre, axis=-1, keepdims=True)
    return centre * lax.rsqrt(spread + norm_eps)


def scaled_norm(values, norm_gain, norm_bias):
    return layer_norm(values) * norm_gain + norm_bias


def modulated(values, head_shift, head_scale):
    return layer_norm(values) * (1.0 + head_scale) + head_shift


def gelu_exact(values):
    return jax.nn.gelu(values, approximate=False)


def matmul(left_side, right_side):
    return jnp.dot(left_side, right_side, preferred_element_type=jnp.float32)


def matmul_left(left_side, right_side):
    return lax.dot_general(
        left_side, right_side, (((0,), (0,)), ((), ())), preferred_element_type=jnp.float32
    )


def matmul_right(left_side, right_side):
    return lax.dot_general(
        left_side, right_side, (((1,), (1,)), ((), ())), preferred_element_type=jnp.float32
    )


def split_heads(tensor):
    return tensor.reshape(tensor.shape[0], HEADS, HEAD_DIM).transpose(1, 0, 2)


def join_heads(tensor):
    return tensor.transpose(1, 0, 2).reshape(tensor.shape[1], HEADS * HEAD_DIM)


def head_forward(stacked, allowed):
    query_rows, key_rows, value_rows = stacked
    scores = jnp.where(
        allowed, matmul_right(query_rows, key_rows) * HEAD_DIM ** (-0.5), masked_fill
    )
    largest = jnp.max(scores, axis=1, keepdims=True)
    powered = jnp.exp(scores - largest)
    totals = jnp.sum(powered, axis=1, keepdims=True)
    weights = (powered / totals).astype(jnp.bfloat16)
    attended = matmul(weights, value_rows).astype(jnp.bfloat16)
    return (attended, (largest + jnp.log(totals))[:, 0])


def head_backward(stacked, allowed):
    query_rows, key_rows, value_rows, log_total, grad_rows = stacked
    scores = jnp.where(
        allowed, matmul_right(query_rows, key_rows) * HEAD_DIM ** (-0.5), masked_fill
    )
    weights = jnp.exp(scores - log_total[:, None])
    grad_weights = matmul_right(grad_rows, value_rows)
    row_inner = jnp.sum(weights * grad_weights, axis=1, keepdims=True)
    grad_scores = (weights * (grad_weights - row_inner)).astype(jnp.bfloat16)
    grad_query = matmul(grad_scores, key_rows) * HEAD_DIM ** (-0.5)
    grad_keys = matmul_left(grad_scores, query_rows) * HEAD_DIM ** (-0.5)
    grad_values = matmul_left(weights.astype(jnp.bfloat16), grad_rows)
    return (grad_query, grad_keys, grad_values)


def adam_step(master, gradient, moment, square, decays, rate):
    new_moment = beta_first * moment + (1.0 - beta_first) * gradient
    new_square = beta_second * square + (1.0 - beta_second) * gradient * gradient
    moment_hat = new_moment / (1.0 - beta_first**STEP)
    square_hat = new_square / (1.0 - beta_second**STEP)
    shrunk = master * (1.0 - rate * weight_decay * decays)
    return (shrunk - rate * moment_hat / (jnp.sqrt(square_hat) + adam_eps), new_moment, new_square)


def average_factors():
    total = 1.0 - ema_decay**STEP
    return (ema_decay * (1.0 - ema_decay ** (STEP - 1)) / total, (1.0 - ema_decay) / total)


def body(
    tokens,
    head_in,
    image_ids,
    out_cotangent,
    head_cotangent,
    weight_attend,
    weight_proj,
    weight_up,
    weight_down,
    weight_cond,
    weight_mod,
    weight_inner,
    weight_outer,
    norm_params,
    mean_attend,
    mean_proj,
    mean_up,
    mean_down,
    mean_cond,
    mean_mod,
    mean_inner,
    mean_outer,
    mean_norms,
    square_attend,
    square_proj,
    square_up,
    square_down,
    square_cond,
    square_mod,
    square_inner,
    square_outer,
    square_norms,
    ema_attend,
    ema_proj,
    ema_up,
    ema_down,
    ema_cond,
    ema_mod,
    ema_inner,
    ema_outer,
    ema_norms,
):
    used = (
        lax.all_gather(
            weight_attend.astype(jnp.bfloat16), ("dp", "side", "seq"), axis=0, tiled=True
        ),
        lax.all_gather(weight_proj.astype(jnp.bfloat16), ("dp", "side", "seq"), axis=0, tiled=True),
        lax.all_gather(weight_up.astype(jnp.bfloat16), ("dp", "side", "seq"), axis=0, tiled=True),
        lax.all_gather(weight_down.astype(jnp.bfloat16), ("dp", "side", "seq"), axis=0, tiled=True),
        lax.all_gather(weight_cond.astype(jnp.bfloat16), ("dp", "side", "seq"), axis=0, tiled=True),
        lax.all_gather(weight_mod.astype(jnp.bfloat16), ("dp", "side", "seq"), axis=0, tiled=True),
        lax.all_gather(
            weight_inner.astype(jnp.bfloat16), ("dp", "side", "seq"), axis=0, tiled=True
        ),
        lax.all_gather(
            weight_outer.astype(jnp.bfloat16), ("dp", "side", "seq"), axis=0, tiled=True
        ),
        lax.all_gather(norm_params.astype(jnp.bfloat16), ("dp", "side", "seq"), axis=0, tiled=True),
    )
    use_attend, use_proj, use_up, use_down, use_cond, use_mod, use_inner, use_outer, use_norms = (
        used
    )
    norm_set = use_norms.astype(jnp.float32)
    inputs = tokens.astype(jnp.float32)
    row_count = tokens.shape[0]
    normed, first_back = jax.vjp(scaled_norm, inputs, norm_set[:, 0], norm_set[:, 1])
    normed_low = normed.astype(jnp.bfloat16)
    mixed_rows = matmul(normed_low, use_attend).astype(jnp.bfloat16)
    query_heads = split_heads(mixed_rows[:, :D])
    own_keys = split_heads(mixed_rows[:, D : 2 * D])
    own_values = split_heads(mixed_rows[:, 2 * D :])
    own_images = image_ids.astype(jnp.bfloat16)
    far_pair, far_images = shifted((mixed_rows[:, D:], own_images), "side", 1)
    both_keys = jnp.concatenate([split_heads(far_pair[:, :D]), own_keys], axis=1)
    both_values = jnp.concatenate([split_heads(far_pair[:, D:]), own_values], axis=1)
    near_allowed = own_images[:, None] == own_images[None, :]
    wide_allowed = own_images[:, None] == jnp.concatenate([far_images, own_images])[None, :]
    masked_side = lax.axis_index("side") == 1

    def visible_forward():
        return lax.map(
            lambda stacked: head_forward(stacked, near_allowed), (query_heads, own_keys, own_values)
        )

    def masked_forward():
        return lax.map(
            lambda stacked: head_forward(stacked, wide_allowed),
            (query_heads, both_keys, both_values),
        )

    attended_heads, log_totals = lax.cond(masked_side, masked_forward, visible_forward)
    attended = join_heads(attended_heads)
    hidden = inputs + matmul(attended, use_proj)
    second, second_back = jax.vjp(scaled_norm, hidden, norm_set[:, 2], norm_set[:, 3])
    second_low = second.astype(jnp.bfloat16)
    inner_pre = matmul(second_low, use_up)
    activated_full, gelu_back = jax.vjp(gelu_exact, inner_pre)
    activated = activated_full.astype(jnp.bfloat16)
    block_low = (hidden + matmul(activated, use_down)).astype(jnp.bfloat16)
    condition = matmul(block_low, use_cond)
    lifted_cond, cond_back = jax.vjp(jax.nn.silu, condition)
    cond_low = lifted_cond.astype(jnp.bfloat16)
    modulation = matmul(cond_low, use_mod)
    head_shift = modulation[:, :HW]
    head_scale = modulation[:, HW : 2 * HW]
    head_gate = modulation[:, 2 * HW :]
    head_rows = head_in.astype(jnp.float32)
    shaped, shaped_back = jax.vjp(modulated, head_rows, head_shift, head_scale)
    shaped_low = shaped.astype(jnp.bfloat16)
    middle = matmul(shaped_low, use_inner)
    lifted_full, middle_back = jax.vjp(jax.nn.silu, middle)
    lifted_rows = lifted_full.astype(jnp.bfloat16)
    branch = matmul(lifted_rows, use_outer)
    head_out = (head_rows + head_gate * branch).astype(jnp.bfloat16)
    head_grad = head_cotangent.astype(jnp.float32)
    grad_branch = (head_grad * head_gate).astype(jnp.bfloat16)
    grad_outer = matmul_left(lifted_rows, grad_branch)
    grad_middle = middle_back(matmul_right(grad_branch, use_outer))[0].astype(jnp.bfloat16)
    grad_inner = matmul_left(shaped_low, grad_middle)
    head_part, grad_shift, grad_scale = shaped_back(matmul_right(grad_middle, use_inner))
    head_in_grad = head_grad + head_part
    grad_modulation = jnp.concatenate([grad_shift, grad_scale, head_grad * branch], axis=1).astype(
        jnp.bfloat16
    )
    grad_mod = matmul_left(cond_low, grad_modulation)
    grad_condition = cond_back(matmul_right(grad_modulation, use_mod))[0].astype(jnp.bfloat16)
    grad_cond = matmul_left(block_low, grad_condition)
    grad_block = out_cotangent.astype(jnp.float32) + matmul_right(grad_condition, use_cond)
    grad_feed = grad_block.astype(jnp.bfloat16)
    grad_down = matmul_left(activated, grad_feed)
    grad_inner_pre = gelu_back(matmul_right(grad_feed, use_down))[0].astype(jnp.bfloat16)
    grad_up = matmul_left(second_low, grad_inner_pre)
    hidden_part, grad_gain_two, grad_bias_two = second_back(matmul_right(grad_inner_pre, use_up))
    grad_hidden = grad_block + hidden_part
    grad_proj_out = grad_hidden.astype(jnp.bfloat16)
    grad_proj = matmul_left(attended, grad_proj_out)
    grad_attended = split_heads(matmul_right(grad_proj_out, use_proj).astype(jnp.bfloat16))

    def visible_backward():
        grad_query, grad_keys, grad_values = lax.map(
            lambda stacked: head_backward(stacked, near_allowed),
            (query_heads, own_keys, own_values, log_totals, grad_attended),
        )
        zero_fill = jnp.zeros_like(grad_keys)
        return (
            grad_query,
            jnp.concatenate([zero_fill, grad_keys], axis=1),
            jnp.concatenate([zero_fill, grad_values], axis=1),
        )

    def masked_backward():
        return lax.map(
            lambda stacked: head_backward(stacked, wide_allowed),
            (query_heads, both_keys, both_values, log_totals, grad_attended),
        )

    grad_query, grad_keys, grad_values = lax.cond(masked_side, masked_backward, visible_backward)
    far_grad = jnp.concatenate(
        [join_heads(grad_keys[:, :row_count]), join_heads(grad_values[:, :row_count])], axis=1
    )
    returned = shifted(far_grad.astype(jnp.bfloat16), "side", -1).astype(far_grad.dtype)
    near_grad = (
        jnp.concatenate(
            [join_heads(grad_keys[:, row_count:]), join_heads(grad_values[:, row_count:])], axis=1
        )
        + returned
    )
    grad_mixed = jnp.concatenate([join_heads(grad_query), near_grad], axis=1).astype(jnp.bfloat16)
    grad_attend = matmul_left(normed_low, grad_mixed)
    tokens_part, grad_gain_one, grad_bias_one = first_back(matmul_right(grad_mixed, use_attend))
    tokens_grad = grad_hidden + tokens_part
    grad_norms = jnp.stack([grad_gain_one, grad_bias_one, grad_gain_two, grad_bias_two], axis=1)
    owned = (
        lax.psum_scatter(grad_attend, ("dp", "side", "seq"), scatter_dimension=0, tiled=True),
        lax.psum_scatter(grad_proj, ("dp", "side", "seq"), scatter_dimension=0, tiled=True),
        lax.psum_scatter(grad_up, ("dp", "side", "seq"), scatter_dimension=0, tiled=True),
        lax.psum_scatter(grad_down, ("dp", "side", "seq"), scatter_dimension=0, tiled=True),
        lax.psum_scatter(grad_cond, ("dp", "side", "seq"), scatter_dimension=0, tiled=True),
        lax.psum_scatter(grad_mod, ("dp", "side", "seq"), scatter_dimension=0, tiled=True),
        lax.psum_scatter(grad_inner, ("dp", "side", "seq"), scatter_dimension=0, tiled=True),
        lax.psum_scatter(grad_outer, ("dp", "side", "seq"), scatter_dimension=0, tiled=True),
        lax.psum_scatter(grad_norms, ("dp", "side", "seq"), scatter_dimension=0, tiled=True),
    )
    local_squares = sum((jnp.sum(gradient * gradient) for gradient in owned))
    grad_norm = jnp.sqrt(lax.psum(local_squares, ("dp", "side", "seq")))
    factor = jnp.minimum(1.0, clip_limit / (grad_norm + 1e-06))
    masters = [
        weight_attend,
        weight_proj,
        weight_up,
        weight_down,
        weight_cond,
        weight_mod,
        weight_inner,
        weight_outer,
        norm_params,
    ]
    moments = [
        mean_attend,
        mean_proj,
        mean_up,
        mean_down,
        mean_cond,
        mean_mod,
        mean_inner,
        mean_outer,
        mean_norms,
    ]
    squares = [
        square_attend,
        square_proj,
        square_up,
        square_down,
        square_cond,
        square_mod,
        square_inner,
        square_outer,
        square_norms,
    ]
    averages = [
        ema_attend,
        ema_proj,
        ema_up,
        ema_down,
        ema_cond,
        ema_mod,
        ema_inner,
        ema_outer,
        ema_norms,
    ]
    keep_old, take_new = average_factors()
    results = []
    smoothed = []
    for position in range(9):
        decays = 1.0 if position < 8 else 0.0
        fresh = adam_step(
            masters[position],
            owned[position] * factor,
            moments[position],
            squares[position],
            decays,
            learn_rates[position],
        )
        results.extend(fresh)
        smoothed.append(keep_old * averages[position] + take_new * fresh[0])
    return (
        (block_low, head_out, tokens_grad, head_in_grad, grad_norm)
        + tuple(results)
        + tuple(smoothed)
    )


def solution(mesh):
    in_specs = (
        P(("dp", "side", "seq"), None),
        P(("dp", "side", "seq"), None),
        P(("dp", "side", "seq")),
        P(("dp", "side", "seq"), None),
        P(("dp", "side", "seq"), None),
        P(("dp", "side", "seq"), None),
        P(("dp", "side", "seq"), None),
        P(("dp", "side", "seq"), None),
        P(("dp", "side", "seq"), None),
        P(("dp", "side", "seq"), None),
        P(("dp", "side", "seq"), None),
        P(("dp", "side", "seq"), None),
        P(("dp", "side", "seq"), None),
        P(("dp", "side", "seq"), None),
        P(("dp", "side", "seq"), None),
        P(("dp", "side", "seq"), None),
        P(("dp", "side", "seq"), None),
        P(("dp", "side", "seq"), None),
        P(("dp", "side", "seq"), None),
        P(("dp", "side", "seq"), None),
        P(("dp", "side", "seq"), None),
        P(("dp", "side", "seq"), None),
        P(("dp", "side", "seq"), None),
        P(("dp", "side", "seq"), None),
        P(("dp", "side", "seq"), None),
        P(("dp", "side", "seq"), None),
        P(("dp", "side", "seq"), None),
        P(("dp", "side", "seq"), None),
        P(("dp", "side", "seq"), None),
        P(("dp", "side", "seq"), None),
        P(("dp", "side", "seq"), None),
        P(("dp", "side", "seq"), None),
        P(("dp", "side", "seq"), None),
        P(("dp", "side", "seq"), None),
        P(("dp", "side", "seq"), None),
        P(("dp", "side", "seq"), None),
        P(("dp", "side", "seq"), None),
        P(("dp", "side", "seq"), None),
        P(("dp", "side", "seq"), None),
        P(("dp", "side", "seq"), None),
        P(("dp", "side", "seq"), None),
    )
    out_specs = (
        P(("dp", "side", "seq"), None),
        P(("dp", "side", "seq"), None),
        P(("dp", "side", "seq"), None),
        P(("dp", "side", "seq"), None),
        P(),
        P(("dp", "side", "seq"), None),
        P(("dp", "side", "seq"), None),
        P(("dp", "side", "seq"), None),
        P(("dp", "side", "seq"), None),
        P(("dp", "side", "seq"), None),
        P(("dp", "side", "seq"), None),
        P(("dp", "side", "seq"), None),
        P(("dp", "side", "seq"), None),
        P(("dp", "side", "seq"), None),
        P(("dp", "side", "seq"), None),
        P(("dp", "side", "seq"), None),
        P(("dp", "side", "seq"), None),
        P(("dp", "side", "seq"), None),
        P(("dp", "side", "seq"), None),
        P(("dp", "side", "seq"), None),
        P(("dp", "side", "seq"), None),
        P(("dp", "side", "seq"), None),
        P(("dp", "side", "seq"), None),
        P(("dp", "side", "seq"), None),
        P(("dp", "side", "seq"), None),
        P(("dp", "side", "seq"), None),
        P(("dp", "side", "seq"), None),
        P(("dp", "side", "seq"), None),
        P(("dp", "side", "seq"), None),
        P(("dp", "side", "seq"), None),
        P(("dp", "side", "seq"), None),
        P(("dp", "side", "seq"), None),
        P(("dp", "side", "seq"), None),
        P(("dp", "side", "seq"), None),
        P(("dp", "side", "seq"), None),
        P(("dp", "side", "seq"), None),
        P(("dp", "side", "seq"), None),
        P(("dp", "side", "seq"), None),
        P(("dp", "side", "seq"), None),
        P(("dp", "side", "seq"), None),
        P(("dp", "side", "seq"), None),
    )
    return jax.shard_map(body, mesh=mesh, in_specs=in_specs, out_specs=out_specs, check_vma=False)
```

profile of v0, /device:TPU:0, one launch (start us, length us, event | category | flops | bytes accessed | tf_op | source)
XLA Modules:
  0.0 1667.1 jit_solution(11212470692192726106)
XLA Ops:
  24.2 68.8 %all-gather = bf16[32,24,4]{1,2,0:T(4,128)(2,1)S(1)} all-gather(bf16[1,24,4]{1,2,0:T(4,128)(2,1)S(1)} %convert_bitcast_fusion), channel_id=1, replica_groups=mesh['dp'=4,'side'=2,'seq'=4] {'dp','side','seq'}, dimensions={0}, use_global_device_ids=true | all-gather | bytes 6336 | tf_op jit(solution)/shard_map/all_gather | solution.py:172
  108.9 29.3 %conditional.2 = (bf16[12,256,64]{1,2,0:T(8,128)(2,1)}, f32[12,256]{1,0:T(8,128)}) conditional(s32[]{:T(128)} %convert_element_type.128, (bf16[12,256,64]{1,2,0:T(8,128)(2,1)S(1)}, bf16[12,256,64]{1,2,0:T(8,128)(2,1)S(1)}, pred[256,256]{0,1:T(32,128)(4,1)S(1)}, bf16[12,256,64]{1,2,0:T(8,128)(2,1)S(1)}) %tuple.211, ...), branch_computations={%region_2.7_spmd, %region_7.12_spmd} | conditional | flops 34619136 | bytes 3485917 | solution.py:205
  108.9 29.3 %while.48 = (s32[]{:T(128)}, bf16[12,256,64]{1,2,0:T(8,128)(2,1)}, f32[12,256]{1,0:T(8,128)}, bf16[12,256,64]{1,2,0:T(8,128)(2,1)S(1)}, bf16[12,256,64]{1,2,0:T(...) while((s32[]{:T(128)}, bf16[12,256,64]{1,2,0:T(8,128)(2,1)}, ...), condition=%wide.region_6.6_spmd, body=%wide.region_3.5_spmd.sunk | while | flops 17317632 | bytes 995425 | solution.py:195
  140.4 56.3 %all-gather.14.cloned.1.call-done = bf16[768,3072]{1,0:T(8,128)(2,1)} async-done(((bf16[24,3072]{1,0:T(8,128)(2,1)}), bf16[768,3072]{1,0:T(8,128)(2,1)}) %all-gather.14.cloned.1.call-update) | async-done | bytes 4718608 | tf_op jit(solution)/shard_map/all_gather | solution.py:162
  196.8 11.6 multiply_convert_fusion.2
  208.4 54.0 %all-gather.16.cloned.1.call-done = bf16[3072,768]{1,0:T(8,128)(2,1)} async-done(((bf16[96,768]{1,0:T(8,128)(2,1)}), bf16[3072,768]{1,0:T(8,128)(2,1)}) %all-gather.16.cloned.1.call-update) | async-done | bytes 4718608 | tf_op jit(solution)/shard_map/all_gather | solution.py:163
  266.6 53.0 %all-gather.18.cloned.1.call-done = bf16[768,1024]{1,0:T(8,128)(2,1)} async-done(((bf16[24,1024]{1,0:T(8,128)(2,1)}), bf16[768,1024]{1,0:T(8,128)(2,1)}) %all-gather.18.cloned.1.call-update) | async-done | bytes 1572880 | tf_op jit(solution)/shard_map/all_gather | solution.py:164
  322.5 68.8 %all-gather.20.cloned.1.call-done = bf16[1024,3072]{1,0:T(8,128)(2,1)} async-done(((bf16[32,3072]{1,0:T(8,128)(2,1)}), bf16[1024,3072]{1,0:T(8,128)(2,1)}) %all-gather.20.cloned.1.call-update) | async-done | bytes 6291472 | tf_op jit(solution)/shard_map/all_gather | solution.py:165
  398.3 51.5 %all-gather.22.cloned.1.call-done = bf16[1024,1024]{1,0:T(8,128)(2,1)} async-done(((bf16[32,1024]{1,0:T(8,128)(2,1)}), bf16[1024,1024]{1,0:T(8,128)(2,1)}) %all-gather.22.cloned.1.call-update) | async-done | bytes 2097168 | tf_op jit(solution)/shard_map/all_gather | solution.py:166
  453.2 55.6 %all-gather.24.cloned.1.call-done = bf16[1024,1024]{1,0:T(8,128)(2,1)} async-done(((bf16[32,1024]{1,0:T(8,128)(2,1)}), bf16[1024,1024]{1,0:T(8,128)(2,1)}) %all-gather.24.cloned.1.call-update) | async-done | bytes 2097168 | tf_op jit(solution)/shard_map/all_gather | solution.py:169
  542.9 85.8 %conditional.3 = (bf16[12,256,64]{1,2,0:T(8,128)(2,1)}, f32[12,512,64]{1,2,0:T(8,128)}, f32[12,512,64]{1,2,0:T(8,128)}) conditional(s32[]{:T(128)} %convert_element_type.128, (bf16[12,256,64]{1,2,0:T(8,128)(2,1)}, bf16[12,256,64]{1,2,0:T(8,128)(2,1)}, pred[256,256]{0,1:T(32,128)(4,1)S(1)}, f32[12,256]{1,0:T(8,128)}, ...), branch_computations={%region_18.22_spmd, %region_22.26_spmd} | conditional | flops 85114624 | bytes 7186673 | solution.py:271
  543.0 80.6 %while.50 = (s32[]{:T(128)}, bf16[12,256,64]{1,2,0:T(8,128)(2,1)}, f32[12,256,64]{1,2,0:T(8,128)}, f32[12,256,64]{1,2,0:T(8,128)}, bf16[12,256,64]{1,2,0:T(8,128...) while((s32[]{:T(128)}, bf16[12,256,64]{1,2,0:T(8,128)(2,1)}, ...), condition=%wide.region_21.21_spmd, body=%wide.region_19.20_spmd.sunk | while | flops 42565376 | bytes 2467953 | solution.py:254
  642.4 6.6 fusion.162
  650.1 6.5 fusion.135
  658.2 7.4 fusion.126
  673.1 39.6 %all-reduce.2 = f32[768,4]{0,1:T(4,128)S(1)} all-reduce(f32[768,4]{0,1:T(4,128)S(1)} %pad_maximum_fusion.11), channel_id=10, replica_groups=mesh['dp'=4,'side'=2,'seq'=4] {'dp','side','seq'}, use_global_device_ids=true, to_apply=%region_50.51.clone | all-reduce | flops 3072 | bytes 24576
  714.8 19.2 %reduce-scatter.18.cloned.1.call-done = f32[24,1024]{1,0:T(8,128)} async-done(((f32[768,1024]{1,0:T(8,128)}), f32[24,1024]{1,0:T(8,128)}) %reduce-scatter.18.cloned.1.call-update) | async-done | bytes 98320 | tf_op jit(solution)/shard_map/reduce_scatter | solution.py:292
  735.5 148.1 %reduce-scatter.22.cloned.1.call-done = f32[32,1024]{1,0:T(8,128)} async-done(((f32[1024,1024]{1,0:T(8,128)}), f32[32,1024]{1,0:T(8,128)}) %reduce-scatter.22.cloned.1.call-update) | async-done | bytes 131088 | tf_op jit(solution)/shard_map/reduce_scatter | solution.py:294
  885.3 147.1 %reduce-scatter.24.cloned.1.call-done = f32[32,1024]{1,0:T(8,128)} async-done(((f32[1024,1024]{1,0:T(8,128)}), f32[32,1024]{1,0:T(8,128)}) %reduce-scatter.24.cloned.1.call-update) | async-done | bytes 131088 | tf_op jit(solution)/shard_map/reduce_scatter | solution.py:295
  1034.0 122.9 %reduce-scatter.10.cloned.1.call-done = f32[24,2304]{1,0:T(8,128)} async-done(((f32[768,2304]{1,0:T(8,128)}), f32[24,2304]{1,0:T(8,128)}) %reduce-scatter.10.cloned.1.call-update) | async-done | bytes 221200 | tf_op jit(solution)/shard_map/reduce_scatter | solution.py:288
  1159.7 137.8 %reduce-scatter.14.cloned.1.call-done = f32[24,3072]{1,0:T(8,128)} async-done(((f32[768,3072]{1,0:T(8,128)}), f32[24,3072]{1,0:T(8,128)}) %reduce-scatter.14.cloned.1.call-update) | async-done | bytes 294928 | tf_op jit(solution)/shard_map/reduce_scatter | solution.py:290
  1299.8 138.8 %reduce-scatter.16.cloned.1.call-done = f32[96,768]{1,0:T(8,128)} async-done(((f32[3072,768]{1,0:T(8,128)}), f32[96,768]{1,0:T(8,128)}) %reduce-scatter.16.cloned.1.call-update) | async-done | bytes 294928 | tf_op jit(solution)/shard_map/reduce_scatter | solution.py:291
  1441.5 157.9 %reduce-scatter.20.cloned.1.call-done = f32[32,3072]{1,0:T(8,128)} async-done(((f32[1024,3072]{1,0:T(8,128)}), f32[32,3072]{1,0:T(8,128)}) %reduce-scatter.20.cloned.1.call-update) | async-done | bytes 393232 | tf_op jit(solution)/shard_map/reduce_scatter | solution.py:293
  1605.0 39.7 %psum.7 = f32[]{:T(128)} all-reduce(f32[]{:T(128)S(6)} %add.338), channel_id=1, replica_groups=mesh['dp'=4,'side'=2,'seq'=4] {'dp','side','seq'}, use_global_device_ids=true, to_apply=%region_52.53 | all-reduce | flops 1 | bytes 8 | tf_op jit(solution)/shard_map/psum | solution.py:299
  (442 shorter events, 252.3 us)
Async XLA Ops:
  7.3 86.6 %all-gather.10.cloned.1.call-start = ((), (), s32[]{:S(2)}) async-start(), calls=%async_computation.8 | async-start | bytes 3649536 | tf_op jit(solution)/shard_map/all_gather | solution.py:158
  9.0 129.2 %all-gather.12.cloned.1.call-start = ((), (), s32[]{:S(2)}) async-start(), calls=%async_computation.9 | async-start | bytes 1216512 | tf_op jit(solution)/shard_map/all_gather | solution.py:161
  10.6 186.2 %all-gather.14.cloned.1.call-start = ((), (), s32[]{:S(2)}) async-start(), calls=%async_computation.10 | async-start | bytes 4866048 | tf_op jit(solution)/shard_map/all_gather | solution.py:162
  12.3 250.1 %all-gather.16.cloned.1.call-start = ((), (), s32[]{:S(2)}) async-start(), calls=%async_computation.11 | async-start | bytes 4866048 | tf_op jit(solution)/shard_map/all_gather | solution.py:163
  14.0 305.6 %all-gather.18.cloned.1.call-start = ((), (), s32[]{:S(2)}) async-start(), calls=%async_computation.12 | async-start | bytes 1622016 | tf_op jit(solution)/shard_map/all_gather | solution.py:164
  15.6 375.8 %all-gather.20.cloned.1.call-start = ((), (), s32[]{:S(2)}) async-start(), calls=%async_computation.13 | async-start | bytes 6488064 | tf_op jit(solution)/shard_map/all_gather | solution.py:165
  17.4 432.5 %all-gather.22.cloned.1.call-start = ((), (), s32[]{:S(2)}) async-start(), calls=%async_computation.14 | async-start | bytes 2162688 | tf_op jit(solution)/shard_map/all_gather | solution.py:166
  19.0 489.8 %all-gather.24.cloned.1.call-start = ((), (), s32[]{:S(2)}) async-start(), calls=%async_computation.15 | async-start | bytes 2162688 | tf_op jit(solution)/shard_map/all_gather | solution.py:169
  19.7 80.5 %collective-permute-start.1 = (bf16[256]{0:T(256)(128)(2,1)S(1)}, bf16[256]{0:T(256)(128)(2,1)S(1)}, u32[]{:S(2)}, u32[]{:S(2)}) collective-permute-start(bf16[256]{0:T(256)(128)(2,1)S(1)} %convert_element_type.134), channel_id=1, source_target_pairs={{0,4},{1,5},{2,6},{3,7},{8,12},{9,13},{10,14},{11,15},{16,20},{17,... | collective-permute-start | bytes 1544 | tf_op jit(solution)/shard_map/ppermute | solution.py:27
  23.6 689.7 %reduce-scatter.12.cloned.1.call-start = ((), (), s32[]{:S(2)}) async-start(), calls=%async_computation.17 | async-start | bytes 2433024 | tf_op jit(solution)/shard_map/reduce_scatter | solution.py:289
  98.0 4.8 collective-permute-start
  529.0 205.0 %reduce-scatter.18.cloned.1.call-start = ((), (), s32[]{:S(2)}) async-start(), calls=%async_computation.20 | async-start | bytes 3244032 | tf_op jit(solution)/shard_map/reduce_scatter | solution.py:292
  532.5 351.1 %reduce-scatter.22.cloned.1.call-start = ((), (), s32[]{:S(2)}) async-start(), calls=%async_computation.22 | async-start | bytes 4325376 | tf_op jit(solution)/shard_map/reduce_scatter | solution.py:294
  535.3 497.0 %reduce-scatter.24.cloned.1.call-start = ((), (), s32[]{:S(2)}) async-start(), calls=%async_computation.23 | async-start | bytes 4325376 | tf_op jit(solution)/shard_map/reduce_scatter | solution.py:295
  540.9 615.9 %reduce-scatter.10.cloned.1.call-start = ((), (), s32[]{:S(2)}) async-start(), calls=%async_computation.16 | async-start | bytes 7299072 | tf_op jit(solution)/shard_map/reduce_scatter | solution.py:288
  631.1 4.8 collective-permute-start.2
  642.3 655.2 %reduce-scatter.14.cloned.1.call-start = ((), (), s32[]{:S(2)}) async-start(), calls=%async_computation.18 | async-start | bytes 9732096 | tf_op jit(solution)/shard_map/reduce_scatter | solution.py:290
  649.0 789.6 %reduce-scatter.16.cloned.1.call-start = ((), (), s32[]{:S(2)}) async-start(), calls=%async_computation.19 | async-start | bytes 9732096 | tf_op jit(solution)/shard_map/reduce_scatter | solution.py:291
  656.6 942.8 %reduce-scatter.20.cloned.1.call-start = ((), (), s32[]{:S(2)}) async-start(), calls=%async_computation.21 | async-start | bytes 12976128 | tf_op jit(solution)/shard_map/reduce_scatter | solution.py:293
  672.5 973.0 %copy-start.63 = (f32[24,4]{0,1:T(4,128)S(1)}, f32[24,4]{0,1:T(4,128)}, u32[]{:S(2)}) copy-start(f32[24,4]{0,1:T(4,128)} %param.93) | copy-start | bytes 1156
  672.5 973.0 %copy-start.64 = (f32[24,4]{0,1:T(4,128)S(1)}, f32[24,4]{0,1:T(4,128)}, u32[]{:S(2)}) copy-start(f32[24,4]{0,1:T(4,128)} %param.75) | copy-start | bytes 1156
  672.5 973.7 %copy-start.35 = (f32[32,1024]{1,0:T(8,128)S(1)}, f32[32,1024]{1,0:T(8,128)}, u32[]{:S(2)}) copy-start(f32[32,1024]{1,0:T(8,128)} %param.65) | copy-start | bytes 393220
  672.5 973.7 %copy-start.58 = (f32[32,1024]{1,0:T(8,128)S(1)}, f32[32,1024]{1,0:T(8,128)}, u32[]{:S(2)}) copy-start(f32[32,1024]{1,0:T(8,128)} %param.92) | copy-start | bytes 393220
  673.0 975.2 %copy-start.36 = (f32[32,1024]{1,0:T(8,128)S(1)}, f32[32,1024]{1,0:T(8,128)}, u32[]{:S(2)}) copy-start(f32[32,1024]{1,0:T(8,128)} %param.64) | copy-start | bytes 393220
  (69 other events, 3585.0 us)
Sparse Core Ops, SparseCore 0:
  11.5 62.9 all-gather.9
  77.8 52.9 all-gather.11
  134.2 62.5 all-gather.13
  200.0 62.3 all-gather.15
  265.7 53.8 all-gather.17
  322.9 68.4 all-gather.19
  394.9 54.9 all-gather.21
  453.4 55.3 all-gather.23
  529.1 97.9 reduce-scatter.11
  633.2 100.7 reduce-scatter.17
  736.4 147.1 reduce-scatter.21
  885.9 146.4 reduce-scatter.23
  1039.0 117.8 reduce-scatter.9
  1162.6 134.9 reduce-scatter.13
  1304.3 134.2 reduce-scatter.15
  1444.5 154.9 reduce-scatter.19
where the time goes:
time: 1680 us; the launch traced here: 1670 us
  waiting for transfers between devices  1210 us (72%)
  matrix products  173 us (10%)
  blocking collectives  148 us (9%)
  local copies, waits for them, and re-layouts  53.2 us (3%)
  other arithmetic  50.2 us (3%)
  between operations  23.1 us (1%)
    reduce_scatter x1, waiting for transfers between devices, body(): lax.psum_scatter(grad_mod, ('dp', 'side', 'seq'), scatter_dimension=0, ti...  158 us
    reduce_scatter x1, waiting for transfers between devices, body(): lax.psum_scatter(grad_inner, ('dp', 'side', 'seq'), scatter_dimension=0,...  148 us
    reduce_scatter x1, waiting for transfers between devices, body(): lax.psum_scatter(grad_outer, ('dp', 'side', 'seq'), scatter_dimension=0,...  147 us
    reduce_scatter x1, waiting for transfers between devices, body(): lax.psum_scatter(grad_down, ('dp', 'side', 'seq'), scatter_dimension=0, t...  139 us
    reduce_scatter x1, waiting for transfers between devices, body(): lax.psum_scatter(grad_up, ('dp', 'side', 'seq'), scatter_dimension=0, til...  138 us
    reduce_scatter x1, waiting for transfers between devices, body(): lax.psum_scatter(grad_attend, ('dp', 'side', 'seq'), scatter_dimension=0,...  123 us
    all_gather x1, waiting for transfers between devices, body(): lax.all_gather(weight_mod.astype(jnp.bfloat16), ('dp', 'side', 'seq'), ax...  68.8 us
    all_gather x1, blocking collectives, body(): lax.all_gather(norm_params.astype(jnp.bfloat16), ('dp', 'side', 'seq'), a...  68.8 us
  transfers between devices with their start and end apart: 19, of which 14 were waited for; matrix products, arithmetic and copies ran while one was open for 14% of the time, Pallas kernels for 0%

commit v1 on v0

--- a/solution.py
+++ b/solution.py
@@ -1,6 +1,8 @@
 import jax
 import jax.numpy as jnp
 from jax import lax
+from jax.experimental import pallas as pl
+from jax.experimental.pallas import tpu as pltpu
 from jax.sharding import PartitionSpec as P
 
 D = 768
@@ -19,6 +21,249 @@
 adam_eps = 1e-08
 ema_decay = 0.9999
 masked_fill = -1e30
+
+
+MESH = pl.DeviceIdType.MESH
+AXES = ("dp", "side", "seq")
+
+
+def places():
+    dp, side, seq = (lax.axis_index(name) for name in AXES)
+    count = lax.axis_size("seq")
+    near = dp + 1 - 2 * lax.rem(dp, 2)
+    far = dp + 2 - 4 * (dp // 2)
+    along = [lax.rem(seq + step, count) for step in range(1, count)]
+    before = [lax.rem(seq + count - step, count) for step in range(1, count)]
+    return dp, side, seq, near, far, along, before
+
+
+def greet(peers):
+    barrier = pltpu.get_barrier_semaphore()
+    for peer in peers:
+        pl.semaphore_signal(barrier, inc=1, device_id=peer, device_id_type=MESH)
+    pl.semaphore_wait(barrier, len(peers))
+
+
+def remote(source, target, send_sem, recv_sem, peer):
+    return pltpu.make_async_remote_copy(
+        src_ref=source,
+        dst_ref=target,
+        send_sem=send_sem,
+        recv_sem=recv_sem,
+        device_id=peer,
+        device_id_type=MESH,
+    )
+
+
+class Gather:
+    def __init__(self, chunks, masters, fulls, own, slabs, joined, sends, recvs, locs):
+        self.chunks, self.masters, self.fulls = chunks, masters, fulls
+        self.own, self.slabs, self.joined = own, slabs, joined
+        self.sends, self.recvs, self.locs = sends, recvs, locs
+        self.dp, self.side, self.seq, self.near, self.far, self.along, self.before = places()
+        self.count = len(self.along) + 1
+        self.started, self.inside = [], {}
+
+    def rows(self, group, dp, side):
+        size = self.count * self.masters[group].shape[0]
+        return pl.multiple_of((dp * 2 + side) * size, 16), size
+
+    def packed(self, group):
+        return self.masters[group].shape[0] % 16 == 0
+
+    def part(self, chunk, start, size):
+        group, first, width = self.chunks[chunk]
+        return self.fulls[group].at[pl.ds(pl.multiple_of(start, 16), size), pl.ds(first, width)]
+
+    def send(self, chunk, which, source, target, peer):
+        copy = remote(source, target, self.sends.at[chunk, which], self.recvs.at[chunk, which], peer)
+        copy.start()
+        self.started.append(copy)
+
+    def arrived(self, chunk, which, target, peer):
+        remote(target, target, self.sends.at[chunk, which], self.recvs.at[chunk, which], peer).wait_recv()
+
+    def local(self, chunk, source, target):
+        copy = pltpu.make_async_copy(source, target, self.locs.at[chunk])
+        copy.start()
+        self.inside[chunk] = copy
+
+    def cast(self, group):
+        rounded = self.masters[group][...].astype(jnp.bfloat16)
+        if self.packed(group):
+            self.own[group][...] = rounded
+        else:
+            self.slabs[group][self.seq] = rounded
+
+    def first(self, chunk):
+        group, start, width = self.chunks[chunk]
+        columns = pl.ds(start, width)
+        rows = self.masters[group].shape[0]
+        base, _ = self.rows(group, self.dp, self.side)
+        for step, peer in enumerate(self.along):
+            if self.packed(group):
+                source = self.own[group].at[:, columns]
+                target = self.part(chunk, base + self.seq * rows, rows)
+            else:
+                source = target = self.slabs[group].at[self.seq, :, columns]
+            self.send(chunk, step, source, target, (self.dp, self.side, peer))
+        if self.packed(group):
+            self.local(chunk, self.own[group].at[:, columns], self.part(chunk, base + self.seq * rows, rows))
+
+    def second(self, chunk):
+        group, start, width = self.chunks[chunk]
+        columns = pl.ds(start, width)
+        rows = self.masters[group].shape[0]
+        base, size = self.rows(group, self.dp, self.side)
+        for step, peer in enumerate(self.before):
+            if self.packed(group):
+                target = self.part(chunk, base + peer * rows, rows)
+            else:
+                target = self.slabs[group].at[peer, :, columns]
+            self.arrived(chunk, step, target, (self.dp, self.side, peer))
+        block = self.part(chunk, base, size)
+        if self.packed(group):
+            self.inside.pop(chunk).wait()
+            source = block
+        else:
+            tile = 256
+            joined, slab = self.joined[group], self.slabs[group]
+
+            @pl.loop(0, width // tile)
+            def _(at):
+                span = pl.ds(pl.multiple_of(start + at * tile, tile), tile)
+                stacked = [slab[place, :, span].astype(jnp.float32) for place in range(self.count)]
+                joined[:, span] = jnp.concatenate(stacked, axis=0).astype(jnp.bfloat16)
+
+            source = joined.at[:, columns]
+            self.local(chunk, source, block)
+        last = self.count - 1
+        self.send(chunk, last, source, block, (self.near, self.side, self.seq))
+        self.send(chunk, last + 1, source, block, (self.far, self.side, self.seq))
+        self.send(chunk, last + 4, source, block, (self.dp, 1 - self.side, self.seq))
+
+    def third(self, chunk):
+        group = self.chunks[chunk][0]
+        last = self.count - 1
+        size = self.rows(group, self.dp, self.side)[1]
+        half = size // 2
+        other = (self.dp, 1 - self.side, self.seq)
+        near, far = ((place, self.side, self.seq) for place in (self.near, self.far))
+        base = self.rows(group, self.near, self.side)[0]
+        block = self.part(chunk, base, size)
+        self.arrived(chunk, last, block, near)
+        piece = self.part(chunk, base, half)
+        self.send(chunk, last + 3, piece, piece, far)
+        self.send(chunk, last + 5, block, block, other)
+        base = self.rows(group, self.far, self.side)[0]
+        block = self.part(chunk, base, size)
+        self.arrived(chunk, last + 1, block, far)
+        piece = self.part(chunk, base + half, half)
+        self.send(chunk, last + 2, piece, piece, near)
+        self.send(chunk, last + 6, block, block, other)
+
+    def fourth(self, chunk):
+        group = self.chunks[chunk][0]
+        last = self.count - 1
+        base, size = self.rows(group, 3 - self.dp, self.side)
+        half = size // 2
+        self.arrived(chunk, last + 3, self.part(chunk, base, half), (self.far, self.side, self.seq))
+        self.arrived(chunk, last + 2, self.part(chunk, base + half, half), (self.near, self.side, self.seq))
+        block = self.part(chunk, base, size)
+        self.send(chunk, last + 7, block, block, (self.dp, 1 - self.side, self.seq))
+
+    def fifth(self, chunk):
+        group = self.chunks[chunk][0]
+        last = self.count - 1
+        other = (self.dp, 1 - self.side, self.seq)
+        for which, place in enumerate((self.dp, self.near, self.far, 3 - self.dp)):
+            base, size = self.rows(group, place, 1 - self.side)
+            self.arrived(chunk, last + 4 + which, self.part(chunk, base, size), other)
+
+    def finish(self):
+        for copy in self.started:
+            copy.wait_send()
+        for copy in self.inside.values():
+            copy.wait()
+
+
+def chunk_list(masters):
+    chunks = []
+    for group, shape in enumerate(masters):
+        rows, width = shape
+        step = width
+        while rows * step > 32 * 1024 and step % 512 == 0:
+            step //= 2
+        if rows * step > 32 * 1024 and step % 384 == 0:
+            step //= 3
+        chunks += [(group, start, step) for start in range(0, width, step)]
+    return chunks
+
+
+def gather_kernel(chunks, *refs):
+    masters, fulls = refs[:8], refs[8:16]
+    rest = list(refs[16:])
+    own, slabs, joined = {}, {}, {}
+    for group in range(8):
+        if masters[group].shape[0] % 16 == 0:
+            own[group] = rest.pop(0)
+        else:
+            slabs[group] = rest.pop(0)
+            joined[group] = rest.pop(0)
+    sends, recvs, locs = rest
+    dp, side, seq, near, far, along, _ = places()
+    peers = [(near, side, seq), (far, side, seq), (dp, 1 - side, seq)]
+    greet(peers + [(dp, side, place) for place in along])
+    flow = Gather(chunks, masters, fulls, own, slabs, joined, sends, recvs, locs)
+    total = len(chunks)
+    for step in range(-2, total + 2):
+        if 0 <= step + 2 < total:
+            group, start, _ = chunks[step + 2]
+            if start == 0:
+                flow.cast(group)
+            flow.first(step + 2)
+        if 0 <= step < total:
+            flow.second(step)
+        if 0 <= step - 1 < total:
+            flow.third(step - 1)
+        if 0 <= step - 2 < total:
+            flow.fourth(step - 2)
+            flow.fifth(step - 2)
+    flow.finish()
+
+
+def gather_all(masters):
+    devices = lax.axis_size("dp") * lax.axis_size("side") * lax.axis_size("seq")
+    count = lax.axis_size("seq")
+    chunks = chunk_list([master.shape for master in masters])
+    scratch = []
+    for master in masters:
+        rows, width = master.shape
+        if rows % 16 == 0:
+            scratch.append(pltpu.VMEM((rows, width), jnp.bfloat16))
+        else:
+            scratch.append(pltpu.VMEM((count, rows, width), jnp.bfloat16))
+            scratch.append(pltpu.VMEM((count * rows, width), jnp.bfloat16))
+    total = len(chunks)
+    scratch += [
+        pltpu.SemaphoreType.DMA((total, count + 7)),
+        pltpu.SemaphoreType.DMA((total, count + 7)),
+        pltpu.SemaphoreType.DMA((total,)),
+    ]
+    vmem, anywhere = pl.BlockSpec(memory_space=pltpu.VMEM), pl.BlockSpec(memory_space=pl.ANY)
+    return pl.pallas_call(
+        lambda *refs: gather_kernel(chunks, *refs),
+        out_shape=[
+            jax.ShapeDtypeStruct((devices * m.shape[0], m.shape[1]), jnp.bfloat16) for m in masters
+        ],
+        in_specs=[vmem] * 8,
+        out_specs=[anywhere] * 8,
+        scratch_shapes=scratch,
+        compiler_params=pltpu.CompilerParams(
+            collective_id=0, has_side_effects=True, vmem_limit_bytes=48 * 2**20
+        ),
+        name="gather",
+    )(*masters)
 
 
 def shifted(value, axis, steps):
@@ -154,26 +399,25 @@
     ema_outer,
     ema_norms,
 ):
-    used = (
-        lax.all_gather(
-            weight_attend.astype(jnp.bfloat16), ("dp", "side", "seq"), axis=0, tiled=True
-        ),
-        lax.all_gather(weight_proj.astype(jnp.bfloat16), ("dp", "side", "seq"), axis=0, tiled=True),
-        lax.all_gather(weight_up.astype(jnp.bfloat16), ("dp", "side", "seq"), axis=0, tiled=True),
-        lax.all_gather(weight_down.astype(jnp.bfloat16), ("dp", "side", "seq"), axis=0, tiled=True),
-        lax.all_gather(weight_cond.astype(jnp.bfloat16), ("dp", "side", "seq"), axis=0, tiled=True),
-        lax.all_gather(weight_mod.astype(jnp.bfloat16), ("dp", "side", "seq"), axis=0, tiled=True),
-        lax.all_gather(
-            weight_inner.astype(jnp.bfloat16), ("dp", "side", "seq"), axis=0, tiled=True
-        ),
-        lax.all_gather(
-            weight_outer.astype(jnp.bfloat16), ("dp", "side", "seq"), axis=0, tiled=True
-        ),
-        lax.all_gather(norm_params.astype(jnp.bfloat16), ("dp", "side", "seq"), axis=0, tiled=True),
-    )
-    use_attend, use_proj, use_up, use_down, use_cond, use_mod, use_inner, use_outer, use_norms = (
-        used
-    )
+    masters = (
+        weight_attend,
+        weight_proj,
+        weight_up,
+        weight_down,
+        weight_cond,
+        weight_mod,
+        weight_inner,
+        weight_outer,
+    )
+    if lax.axis_size("dp") == 4 and lax.axis_size("side") == 2 and weight_attend.shape[0] % 8 == 0:
+        gathered = gather_all(masters)
+    else:
+        gathered = [
+            lax.all_gather(master.astype(jnp.bfloat16), AXES, axis=0, tiled=True)
+            for master in masters
+        ]
+    use_attend, use_proj, use_up, use_down, use_cond, use_mod, use_inner, use_outer = gathered
+    use_norms = lax.all_gather(norm_params.astype(jnp.bfloat16), AXES, axis=0, tiled=True)
     norm_set = use_norms.astype(jnp.float32)
     inputs = tokens.astype(jnp.float32)
     row_count = tokens.shape[0]

time: 1680 us -> 1470 us (0.88)
  waiting for transfers between devices: 1210 us -> 897 us
  Pallas kernels: 0 us -> 117 us
    all_gather x8 -> x0, waiting for transfers between devices: 339 us -> none  [the longest x1 68.8 us: body(): lax.all_gather(weight_mod.astype(jnp.bfloat16), ('dp', 'side', 'seq'), ax...]
    pallas_call x0 -> x1, Pallas kernels: none -> 117 us  [gather_all(): pl.pallas_call(lambda *refs: gather_kernel(chunks, *refs), out_shape=[jax...]
    ppermute x3, waiting for transfers between devices: 1.11 us -> 23.2 us  [shifted(): lax.ppermute(value, axis, [(source, source + steps) for source in range(f...]
  transfers between devices with their start and end apart: 19 -> 11, of which waited for: 14 -> 8; matrix products, arithmetic and copies ran while one was open for 14% -> 9% of each run, Pallas kernels for 0% -> 0%
where the time goes in v1:
time: 1470 us; the launch traced here: 1460 us
  waiting for transfers between devices  897 us (61%)
  matrix products  161 us (11%)
  blocking collectives  150 us (10%)
  Pallas kernels  117 us (8%)
  local copies, waits for them, and re-layouts  62.6 us (4%)
  other arithmetic  39.5 us (3%)
  between operations  23.4 us (2%)
    reduce_scatter x1, waiting for transfers between devices, body(): lax.psum_scatter(grad_mod, ('dp', 'side', 'seq'), scatter_dimension=0, ti...  158 us
    reduce_scatter x1, waiting for transfers between devices, body(): lax.psum_scatter(grad_inner, ('dp', 'side', 'seq'), scatter_dimension=0,...  148 us
    reduce_scatter x1, waiting for transfers between devices, body(): lax.psum_scatter(grad_outer, ('dp', 'side', 'seq'), scatter_dimension=0,...  148 us
    reduce_scatter x1, waiting for transfers between devices, body(): lax.psum_scatter(grad_down, ('dp', 'side', 'seq'), scatter_dimension=0, t...  139 us
    reduce_scatter x1, waiting for transfers between devices, body(): lax.psum_scatter(grad_up, ('dp', 'side', 'seq'), scatter_dimension=0, til...  138 us
    reduce_scatter x1, waiting for transfers between devices, body(): lax.psum_scatter(grad_attend, ('dp', 'side', 'seq'), scatter_dimension=0,...  122 us
    pallas_call x1, Pallas kernels, gather_all(): pl.pallas_call(lambda *refs: gather_kernel(chunks, *refs), out_shape=[jax...  117 us
    all_gather x1, blocking collectives, body(): lax.all_gather(norm_params.astype(jnp.bfloat16), AXES, axis=0, tiled=True)  69.8 us
  transfers between devices with their start and end apart: 11, of which 8 were waited for; matrix products, arithmetic and copies ran while one was open for 9% of the time, Pallas kernels for 0%

profile of v1, /device:TPU:0, one launch (start us, length us, event | category | flops | bytes accessed | tf_op | source)
XLA Modules:
  0.0 1457.0 jit_solution(370320880063590604)
XLA Ops:
  10.4 69.8 %all-gather = bf16[32,24,4]{1,2,0:T(4,128)(2,1)S(1)} all-gather(bf16[1,24,4]{1,2,0:T(4,128)(2,1)S(1)} %convert_bitcast_fusion), channel_id=1, replica_groups=mesh['dp'=4,'side'=2,'seq'=4] {'dp','side','seq'}, dimensions={0}, use_global_device_ids=true | all-gather | bytes 6336 | tf_op jit(solution)/shard_map/all_gather | solution.py:420
  87.9 116.9 %gather.1 = (bf16[768,2304]{1,0:T(8,128)(2,1)}, bf16[768,768]{1,0:T(8,128)(2,1)S(1)}, bf16[768,3072]{1,0:T(8,128)(2,1)}, bf16[3072,768]{1,0:T(8,128)(2,1)}, bf16...) custom-call(f32[24,2304]{1,0:T(8,128)S(1)} %copy-done.6, ...), custom_call_target="tpu_custom_call" | custom-call | tf_op jit(solution)/shard_map/gather/pallas_call | solution.py:254
  229.6 47.6 %conditional.2 = (bf16[12,256,64]{1,2,0:T(8,128)(2,1)}, f32[12,256]{1,0:T(8,128)}) conditional(s32[]{:T(128)} %convert_element_type.104, (bf16[12,256,64]{1,2,0:T(8,128)(2,1)}, bf16[12,256,64]{1,2,0:T(8,128)(2,1)S(1)}, pred[256,256]{0,1:T(32,128)(4,1)S(1)}, bf16[12,256,64]{1,2,0:T(8,128)(2,1)}) %tuple.190, (bf16[12,256,64]{1,2,0:T(8,128)(2,1)}, ...), branch_computations={%region_2.7_spmd, %region_7.12_spmd} | conditional | flops 34619136 | bytes 1913025 | solution.py:449
  229.6 47.4 %while.48 = (s32[]{:T(128)}, bf16[12,256,64]{1,2,0:T(8,128)(2,1)}, f32[12,256]{1,0:T(8,128)}, bf16[12,256,64]{1,2,0:T(8,128)(2,1)}, bf16[12,256,64]{1,2,0:T(8,12...) while((s32[]{:T(128)}, bf16[12,256,64]{1,2,0:T(8,128)(2,1)}, ...), condition=%wide.region_6.6_spmd, body=%wide.region_3.5_spmd.sunk | while | flops 17317632 | bytes 995425 | solution.py:439
  279.3 10.4 multiply_convert_fusion.2
  312.0 3.4 fusion.185
  319.4 4.3 fusion.153
  324.5 68.4 %conditional.3 = (bf16[12,256,64]{1,2,0:T(8,128)(2,1)}, f32[12,512,64]{1,2,0:T(8,128)}, f32[12,512,64]{1,2,0:T(8,128)}) conditional(s32[]{:T(128)} %convert_element_type.104, (bf16[12,256,64]{1,2,0:T(8,128)(2,1)}, bf16[12,256,64]{1,2,0:T(8,128)(2,1)}, pred[256,256]{0,1:T(32,128)(4,1)S(1)}, f32[12,256]{1,0:T(8,128)}, ...), branch_computations={%region_18.22_spmd, %region_22.26_spmd} | conditional | flops 85114624 | bytes 7186673 | solution.py:515
  324.5 65.6 %while.50 = (s32[]{:T(128)}, bf16[12,256,64]{1,2,0:T(8,128)(2,1)}, f32[12,256,64]{1,2,0:T(8,128)S(1)}, f32[12,256,64]{1,2,0:T(8,128)S(1)}, bf16[12,256,64]{1,2,0...) while((s32[]{:T(128)}, bf16[12,256,64]{1,2,0:T(8,128)(2,1)}, ...), condition=%wide.region_21.21_spmd, body=%wide.region_19.20_spmd.sunk | while | flops 42565376 | bytes 2467953 | solution.py:498
  399.1 23.2 %collective-permute-done.2 = bf16[256,1536]{0,1:T(8,128)(2,1)S(1)} collective-permute-done((bf16[256,1536]{0,1:T(8,128)(2,1)S(1)}, bf16[256,1536]{0,1:T(8,128)(2,1)S(1)}, u32[]{:S(2)}, u32[]{:S(2)}) %collective-permute-start.2) | collective-permute-done | bytes 786464 | tf_op jit(solution)/shard_map/ppermute | solution.py:272
  423.4 5.5 fusion.124
  430.1 6.6 fusion.162
  437.8 6.5 fusion.135
  445.7 7.6 fusion.126
  455.8 3.7 fusion.123
  460.1 40.3 %all-reduce.2 = f32[768,4]{0,1:T(4,128)S(1)} all-reduce(f32[768,4]{0,1:T(4,128)S(1)} %pad_maximum_fusion.11), channel_id=10, replica_groups=mesh['dp'=4,'side'=2,'seq'=4] {'dp','side','seq'}, use_global_device_ids=true, to_apply=%region_50.51.clone | all-reduce | flops 3072 | bytes 24576
  502.5 21.4 %reduce-scatter.18.cloned.1.call-done = f32[24,1024]{1,0:T(8,128)} async-done(((f32[768,1024]{1,0:T(8,128)}), f32[24,1024]{1,0:T(8,128)}) %reduce-scatter.18.cloned.1.call-update) | async-done | bytes 98320 | tf_op jit(solution)/shard_map/reduce_scatter | solution.py:536
  525.5 147.6 %reduce-scatter.22.cloned.1.call-done = f32[32,1024]{1,0:T(8,128)} async-done(((f32[1024,1024]{1,0:T(8,128)}), f32[32,1024]{1,0:T(8,128)}) %reduce-scatter.22.cloned.1.call-update) | async-done | bytes 131088 | tf_op jit(solution)/shard_map/reduce_scatter | solution.py:538
  674.7 147.5 %reduce-scatter.24.cloned.1.call-done = f32[32,1024]{1,0:T(8,128)} async-done(((f32[1024,1024]{1,0:T(8,128)}), f32[32,1024]{1,0:T(8,128)}) %reduce-scatter.24.cloned.1.call-update) | async-done | bytes 131088 | tf_op jit(solution)/shard_map/reduce_scatter | solution.py:539
  823.9 122.2 %reduce-scatter.10.cloned.1.call-done = f32[24,2304]{1,0:T(8,128)} async-done(((f32[768,2304]{1,0:T(8,128)}), f32[24,2304]{1,0:T(8,128)}) %reduce-scatter.10.cloned.1.call-update) | async-done | bytes 221200 | tf_op jit(solution)/shard_map/reduce_scatter | solution.py:532
  949.0 137.7 %reduce-scatter.14.cloned.1.call-done = f32[24,3072]{1,0:T(8,128)} async-done(((f32[768,3072]{1,0:T(8,128)}), f32[24,3072]{1,0:T(8,128)}) %reduce-scatter.14.cloned.1.call-update) | async-done | bytes 294928 | tf_op jit(solution)/shard_map/reduce_scatter | solution.py:534
  1089.0 139.2 %reduce-scatter.16.cloned.1.call-done = f32[96,768]{1,0:T(8,128)} async-done(((f32[3072,768]{1,0:T(8,128)}), f32[96,768]{1,0:T(8,128)}) %reduce-scatter.16.cloned.1.call-update) | async-done | bytes 294928 | tf_op jit(solution)/shard_map/reduce_scatter | solution.py:535
  1231.2 157.8 %reduce-scatter.20.cloned.1.call-done = f32[32,3072]{1,0:T(8,128)} async-done(((f32[1024,3072]{1,0:T(8,128)}), f32[32,3072]{1,0:T(8,128)}) %reduce-scatter.20.cloned.1.call-update) | async-done | bytes 393232 | tf_op jit(solution)/shard_map/reduce_scatter | solution.py:537
  1394.5 39.8 %psum.7 = f32[]{:T(128)} all-reduce(f32[]{:T(128)S(6)} %add.338), channel_id=1, replica_groups=mesh['dp'=4,'side'=2,'seq'=4] {'dp','side','seq'}, use_global_device_ids=true, to_apply=%region_52.53 | all-reduce | flops 1 | bytes 8 | tf_op jit(solution)/shard_map/psum | solution.py:543
  (421 shorter events, 221.6 us)
Async XLA Ops:
  7.2 493.8 %reduce-scatter.12.cloned.1.call-start = ((), (), s32[]{:S(2)}) async-start(), calls=%async_computation.9 | async-start | bytes 2433024 | tf_op jit(solution)/shard_map/reduce_scatter | solution.py:533
  209.1 12.0 collective-permute-start
  212.3 8.6 collective-permute-start.1
  311.9 212.1 %reduce-scatter.18.cloned.1.call-start = ((), (), s32[]{:S(2)}) async-start(), calls=%async_computation.12 | async-start | bytes 3244032 | tf_op jit(solution)/shard_map/reduce_scatter | solution.py:536
  315.4 357.7 %reduce-scatter.22.cloned.1.call-start = ((), (), s32[]{:S(2)}) async-start(), calls=%async_computation.14 | async-start | bytes 4325376 | tf_op jit(solution)/shard_map/reduce_scatter | solution.py:538
  318.2 504.0 %reduce-scatter.24.cloned.1.call-start = ((), (), s32[]{:S(2)}) async-start(), calls=%async_computation.15 | async-start | bytes 4325376 | tf_op jit(solution)/shard_map/reduce_scatter | solution.py:539
  323.7 622.4 %reduce-scatter.10.cloned.1.call-start = ((), (), s32[]{:S(2)}) async-start(), calls=%async_computation.8 | async-start | bytes 7299072 | tf_op jit(solution)/shard_map/reduce_scatter | solution.py:532
  395.3 27.0 %collective-permute-start.2 = (bf16[256,1536]{0,1:T(8,128)(2,1)S(1)}, bf16[256,1536]{0,1:T(8,128)(2,1)S(1)}, u32[]{:S(2)}, u32[]{:S(2)}) collective-permute-start(bf16[256,1536]{0,1:T(8,128)(2,1)S(1)} %pad_maximum_fusion.4), channel_id=1, source_target_pairs={{4,0},{5,1},{6,2},{7,3},{12,8},{13,9},{14,10},{15,11},{20,16},{21,... | collective-permute-start | bytes 2359304 | tf_op jit(solution)/shard_map/ppermute | solution.py:272
  429.0 657.8 %reduce-scatter.14.cloned.1.call-start = ((), (), s32[]{:S(2)}) async-start(), calls=%async_computation.10 | async-start | bytes 9732096 | tf_op jit(solution)/shard_map/reduce_scatter | solution.py:534
  436.7 791.6 %reduce-scatter.16.cloned.1.call-start = ((), (), s32[]{:S(2)}) async-start(), calls=%async_computation.11 | async-start | bytes 9732096 | tf_op jit(solution)/shard_map/reduce_scatter | solution.py:535
  444.3 944.6 %reduce-scatter.20.cloned.1.call-start = ((), (), s32[]{:S(2)}) async-start(), calls=%async_computation.13 | async-start | bytes 12976128 | tf_op jit(solution)/shard_map/reduce_scatter | solution.py:537
  459.5 975.5 %copy-start.67 = (f32[24,4]{0,1:T(4,128)S(1)}, f32[24,4]{0,1:T(4,128)}, u32[]{:S(2)}) copy-start(f32[24,4]{0,1:T(4,128)} %param.66) | copy-start | bytes 1156
  459.5 975.5 %copy-start.68 = (f32[24,4]{0,1:T(4,128)S(1)}, f32[24,4]{0,1:T(4,128)}, u32[]{:S(2)}) copy-start(f32[24,4]{0,1:T(4,128)} %param.93) | copy-start | bytes 1156
  459.5 975.5 %copy-start.69 = (f32[24,4]{0,1:T(4,128)S(1)}, f32[24,4]{0,1:T(4,128)}, u32[]{:S(2)}) copy-start(f32[24,4]{0,1:T(4,128)} %param.75) | copy-start | bytes 1156
  459.5 975.5 %copy-start.70 = (f32[24,4]{0,1:T(4,128)S(1)}, f32[24,4]{0,1:T(4,128)}, u32[]{:S(2)}) copy-start(f32[24,4]{0,1:T(4,128)} %param.84) | copy-start | bytes 1156
  459.5 976.2 %copy-start.9 = (f32[32,1024]{1,0:T(8,128)S(1)}, f32[32,1024]{1,0:T(8,128)}, u32[]{:S(2)}) copy-start(f32[32,1024]{1,0:T(8,128)} %refs_7_.1) | copy-start | bytes 393220
  460.0 977.8 %copy-start.11 = (f32[32,1024]{1,0:T(8,128)S(1)}, f32[32,1024]{1,0:T(8,128)}, u32[]{:S(2)}) copy-start(f32[32,1024]{1,0:T(8,128)} %refs_6_.1) | copy-start | bytes 393220
  673.1 764.7 %copy-start.44 = (f32[32,1024]{1,0:T(8,128)S(1)}, f32[32,1024]{1,0:T(8,128)}, u32[]{:S(2)}) copy-start(f32[32,1024]{1,0:T(8,128)} %reduce-scatter.22.cloned.1.call-done) | copy-start | bytes 393220
  822.3 613.5 %copy-start.45 = (f32[32,1024]{1,0:T(8,128)S(1)}, f32[32,1024]{1,0:T(8,128)}, u32[]{:S(2)}) copy-start(f32[32,1024]{1,0:T(8,128)} %reduce-scatter.24.cloned.1.call-done) | copy-start | bytes 393220
  823.9 615.8 %copy-start.1 = (f32[32,3072]{1,0:T(8,128)S(1)}, f32[32,3072]{1,0:T(8,128)}, u32[]{:S(2)}) copy-start(f32[32,3072]{1,0:T(8,128)} %refs_5_.1) | copy-start | bytes 1179652
  1389.0 50.7 %copy-start.33 = (f32[32,3072]{1,0:T(8,128)S(1)}, f32[32,3072]{1,0:T(8,128)}, u32[]{:S(2)}) copy-start(f32[32,3072]{1,0:T(8,128)} %reduce-scatter.20.cloned.1.call-done) | copy-start | bytes 1179652
  1394.5 47.9 %copy-start.51 = (f32[24,1024]{1,0:T(8,128)S(1)}, f32[24,1024]{1,0:T(8,128)}, u32[]{:S(2)}) copy-start(f32[24,1024]{1,0:T(8,128)} %reduce-scatter.18.cloned.1.call-done) | copy-start | bytes 294916
  1394.5 47.9 %copy-start.62 = (f32[24,1024]{1,0:T(8,128)S(1)}, f32[24,1024]{1,0:T(8,128)}, u32[]{:S(2)}) copy-start(f32[24,1024]{1,0:T(8,128)} %param.89) | copy-start | bytes 294916
  1394.5 47.9 %copy-start.63 = (f32[24,1024]{1,0:T(8,128)S(1)}, f32[24,1024]{1,0:T(8,128)}, u32[]{:S(2)}) copy-start(f32[24,1024]{1,0:T(8,128)} %param.71) | copy-start | bytes 294916
  (66 other events, 370.3 us)
Sparse Core Ops, SparseCore 0:
  312.0 104.3 reduce-scatter.11
  422.7 101.2 reduce-scatter.17
  526.4 146.7 reduce-scatter.21
  675.4 146.8 reduce-scatter.23
  828.7 117.3 reduce-scatter.9
  951.9 134.8 reduce-scatter.13
  1093.6 134.5 reduce-scatter.15
  1234.3 154.6 reduce-scatter.19

commit v2 on v1

--- a/solution.py
+++ b/solution.py
@@ -1,3 +1,6 @@
+import functools
+from types import SimpleNamespace
+
 import jax
 import jax.numpy as jnp
 from jax import lax
@@ -21,7 +24,6 @@
 adam_eps = 1e-08
 ema_decay = 0.9999
 masked_fill = -1e30
-
 
 MESH = pl.DeviceIdType.MESH
 AXES = ("dp", "side", "seq")
@@ -200,72 +202,6 @@
     return chunks
 
 
-def gather_kernel(chunks, *refs):
-    masters, fulls = refs[:8], refs[8:16]
-    rest = list(refs[16:])
-    own, slabs, joined = {}, {}, {}
-    for group in range(8):
-        if masters[group].shape[0] % 16 == 0:
-            own[group] = rest.pop(0)
-        else:
-            slabs[group] = rest.pop(0)
-            joined[group] = rest.pop(0)
-    sends, recvs, locs = rest
-    dp, side, seq, near, far, along, _ = places()
-    peers = [(near, side, seq), (far, side, seq), (dp, 1 - side, seq)]
-    greet(peers + [(dp, side, place) for place in along])
-    flow = Gather(chunks, masters, fulls, own, slabs, joined, sends, recvs, locs)
-    total = len(chunks)
-    for step in range(-2, total + 2):
-        if 0 <= step + 2 < total:
-            group, start, _ = chunks[step + 2]
-            if start == 0:
-                flow.cast(group)
-            flow.first(step + 2)
-        if 0 <= step < total:
-            flow.second(step)
-        if 0 <= step - 1 < total:
-            flow.third(step - 1)
-        if 0 <= step - 2 < total:
-            flow.fourth(step - 2)
-            flow.fifth(step - 2)
-    flow.finish()
-
-
-def gather_all(masters):
-    devices = lax.axis_size("dp") * lax.axis_size("side") * lax.axis_size("seq")
-    count = lax.axis_size("seq")
-    chunks = chunk_list([master.shape for master in masters])
-    scratch = []
-    for master in masters:
-        rows, width = master.shape
-        if rows % 16 == 0:
-            scratch.append(pltpu.VMEM((rows, width), jnp.bfloat16))
-        else:
-            scratch.append(pltpu.VMEM((count, rows, width), jnp.bfloat16))
-            scratch.append(pltpu.VMEM((count * rows, width), jnp.bfloat16))
-    total = len(chunks)
-    scratch += [
-        pltpu.SemaphoreType.DMA((total, count + 7)),
-        pltpu.SemaphoreType.DMA((total, count + 7)),
-        pltpu.SemaphoreType.DMA((total,)),
-    ]
-    vmem, anywhere = pl.BlockSpec(memory_space=pltpu.VMEM), pl.BlockSpec(memory_space=pl.ANY)
-    return pl.pallas_call(
-        lambda *refs: gather_kernel(chunks, *refs),
-        out_shape=[
-            jax.ShapeDtypeStruct((devices * m.shape[0], m.shape[1]), jnp.bfloat16) for m in masters
-        ],
-        in_specs=[vmem] * 8,
-        out_specs=[anywhere] * 8,
-        scratch_shapes=scratch,
-        compiler_params=pltpu.CompilerParams(
-            collective_id=0, has_side_effects=True, vmem_limit_bytes=48 * 2**20
-        ),
-        name="gather",
-    )(*masters)
-
-
 def shifted(value, axis, steps):
     count = lax.axis_size(axis)
     first, last = (max(0, -steps), min(count, count - steps))
@@ -356,7 +292,1243 @@
     return (ema_decay * (1.0 - ema_decay ** (STEP - 1)) / total, (1.0 - ema_decay) / total)
 
 
-def body(
+def norm_rows(values):
+    centre = values - jnp.mean(values, axis=-1, keepdims=True)
+    spread = jnp.mean(centre * centre, axis=-1, keepdims=True)
+    scale = lax.rsqrt(spread + norm_eps)
+    return centre * scale, scale
+
+
+def span(at, size):
+    return pl.ds(pl.multiple_of(at * size, size), size)
+
+
+class Moves:
+    def __init__(self, sems):
+        self.sems, self.used, self.open = sems, 0, []
+
+    def start(self, source, target):
+        copy = pltpu.make_async_copy(source, target, self.sems.at[self.used])
+        self.used += 1
+        copy.start()
+        self.open.append(copy)
+        return copy
+
+    def finish(self):
+        for copy in self.open:
+            copy.wait()
+        self.open = []
+
+
+class Swaps:
+    def __init__(self, sends, recvs):
+        self.sends, self.recvs, self.used, self.open = sends, recvs, 0, []
+
+    def start(self, source, target, peer):
+        copy = remote(source, target, self.sends.at[self.used], self.recvs.at[self.used], peer)
+        self.used += 1
+        copy.start()
+        self.open.append(copy)
+        return copy
+
+    def finish(self):
+        for copy in self.open:
+            copy.wait_send()
+        self.open = []
+
+
+def relative(dp, near, far):
+    return (dp, near, far, 3 - dp)
+
+
+class LineSum:
+    def __init__(self, box, swaps):
+        self.box, self.swaps = box, swaps
+        dp, side, seq, near, far, along, _ = places()
+        self.count = len(along) + 1
+        self.spots = (seq, self.count + dp * 2 + side)
+        self.hops = (
+            [(dp, side, place) for place in along],
+            [(place, side, seq) for place in (near, far, 3 - dp)]
+            + [(place, 1 - side, seq) for place in (dp, near, far, 3 - dp)],
+        )
+        self.waiting = []
+        self.level = 0
+
+    def launch(self, value):
+        spot = self.spots[self.level]
+        self.box[spot] = value
+        for peer in self.hops[self.level]:
+            self.waiting.append(self.swaps.start(self.box.at[spot], self.box.at[spot], peer))
+
+    def land(self):
+        for copy in self.waiting:
+            copy.wait_recv()
+        first, size = ((0, self.count), (self.count, 8))[self.level]
+        total = self.box[first]
+        for place in range(first + 1, first + size):
+            total = total + self.box[place]
+        self.waiting = []
+        self.level += 1
+        return total
+
+
+def all_peers():
+    dp, side, seq, near, far, along, _ = places()
+    peers = [(place, side, seq) for place in (near, far, 3 - dp)]
+    peers += [(place, 1 - side, seq) for place in (dp, near, far, 3 - dp)]
+    return peers + [(dp, side, place) for place in along]
+
+
+AHEAD_SEQ = 2
+AHEAD_DP = 0
+TASKS = 3
+
+
+FORWARD_OUT = (
+    ("block_low", D, jnp.bfloat16),
+    ("head_out", HW, jnp.bfloat16),
+    ("grad_branch", HW, jnp.bfloat16),
+    ("grad_gate", HW, jnp.bfloat16),
+    ("scale", HW, jnp.float32),
+    ("slope_middle", HW, jnp.bfloat16),
+    ("slope_cond", HW, jnp.bfloat16),
+    ("slope_inner", 4 * D, jnp.bfloat16),
+    ("hidden", D, jnp.float32),
+    ("mixed", 3 * D, jnp.bfloat16),
+    ("far_pair", 2 * D, jnp.bfloat16),
+)
+FORWARD_LOCAL = (
+    ("normed", D, jnp.bfloat16),
+    ("attended", D, jnp.bfloat16),
+    ("second", D, jnp.bfloat16),
+    ("activated", 4 * D, jnp.bfloat16),
+    ("cond_low", HW, jnp.bfloat16),
+    ("shift", HW, jnp.float32),
+    ("gate", HW, jnp.float32),
+    ("head_norm", HW, jnp.float32),
+    ("shaped", HW, jnp.bfloat16),
+    ("lifted", HW, jnp.bfloat16),
+)
+
+
+def head_mask(which):
+    lane = lax.broadcasted_iota(jnp.int32, (1, 2 * HEAD_DIM), 1)
+    inside = lane < HEAD_DIM if which == 0 else lane >= HEAD_DIM
+    return jnp.where(inside, 1.0, 0.0).astype(jnp.bfloat16)
+
+
+def softmax_columns(keys, queries, bias):
+    scores = matmul_right(keys, queries) * HEAD_DIM ** (-0.5) + bias
+    powered = jnp.exp(scores - jnp.max(scores, axis=0, keepdims=True))
+    return powered / jnp.sum(powered, axis=0, keepdims=True)
+
+
+def fill_bias(bias, far_row, own_row, side):
+    rows = own_row.shape[-1]
+    row = own_row[0:1, :]
+
+    def column(ref):
+        return jnp.broadcast_to(ref[0:1, :], (128, rows)).T[:, 0:1]
+
+    near = column(own_row) == row
+    wide = jnp.logical_and(column(far_row) == row, side == 1)
+    bias[pl.ds(0, rows), :] = jnp.where(wide, 0.0, masked_fill)
+    bias[pl.ds(rows, rows), :] = jnp.where(near, 0.0, masked_fill)
+
+
+def pair_slices(mixed, far_pair, at):
+    width = 2 * HEAD_DIM
+    queries = mixed[:, span(at, width)]
+    second = span(at + D // width, width)
+    third = span(at + 2 * (D // width), width)
+    keys = jnp.concatenate([far_pair[:, span(at, width)], mixed[:, second]], axis=0)
+    values = jnp.concatenate([far_pair[:, second], mixed[:, third]], axis=0)
+    return queries, keys, values
+
+
+def forward_kernel(chunks, count, *refs):
+    rest = list(refs)
+
+    def take(number):
+        taken = rest[:number]
+        del rest[:number]
+        return taken
+
+    masters = take(8)
+    tokens, head_in, head_cotangent, ids, norm_rows_own = take(5)
+    fulls, sides = take(8), take(8)
+    outs = dict(zip([name for name, _, _ in FORWARD_OUT], take(len(FORWARD_OUT))))
+    bias_out, norms_out = take(2)
+    weights = take(8)
+    v = SimpleNamespace(**dict(zip([name for name, _, _ in FORWARD_OUT + FORWARD_LOCAL], take(21))))
+    bias, own_row, far_row, box, norms = take(5)
+    turned = take(3)
+    own, slabs, joined = {}, {}, {}
+    for group in range(8):
+        if masters[group].shape[0] % 16 == 0:
+            own[group] = rest.pop(0)
+        else:
+            slabs[group] = rest.pop(0)
+            joined[group] = rest.pop(0)
+    sends, recvs, locs, loads, moves_sem, swap_send, swap_recv, turn_sem, turn_send, turn_recv = rest
+
+    dp, side, seq, near, far, along, _ = places()
+    other = (dp, 1 - side, seq)
+    greet(all_peers())
+    flow = Gather(chunks, masters, fulls, own, slabs, joined, sends, recvs, locs)
+    moves = Moves(moves_sem)
+    swaps = Swaps(swap_send, swap_recv)
+    line = LineSum(box, swaps)
+    place = (dp * 2 + side) * count + seq
+    width = norm_rows_own.shape[1]
+    norms[...] = jnp.zeros(norms.shape, jnp.float32)
+    norms[0:4, 0:width] = norm_rows_own[...].astype(jnp.bfloat16).astype(jnp.float32)
+    spread = pltpu.roll(norms[...], place * width, 1)
+    own_row[...] = jnp.broadcast_to(ids[...], own_row.shape).astype(jnp.float32)
+    rows = tokens.shape[0]
+    loading = {}
+    turning = {0: [], 1: [], 2: []}
+    landing = []
+
+    def load(chunk):
+        group, start, width = chunks[chunk]
+        columns = pl.ds(start, width)
+        if chunk in flow.inside:
+            flow.inside.pop(chunk).wait()
+        copy = pltpu.make_async_copy(
+            fulls[group].at[:, columns], weights[group].at[:, columns], loads.at[chunk]
+        )
+        copy.start()
+        loading[chunk] = copy
+
+    def put(name):
+        moves.start(getattr(v, name), outs[name])
+
+    def share(group, source, which, done=False):
+        depth = source.shape[0] if done else source.shape[1]
+        buffer = turned[which]
+        if not done:
+            free(which)
+
+            @pl.loop(0, depth // 256)
+            def _(at):
+                buffer[span(at, 256), :] = source[:, span(at, 256)].T
+
+        size = depth // 8
+        for place, block in enumerate(relative(dp, near, far)):
+            mine = pl.multiple_of((block * 2 + side) * size, 16)
+            theirs = pl.multiple_of((block * 2 + 1 - side) * size, 16)
+            into = pl.ds(place * size, size)
+            kept = pltpu.make_async_copy(
+                buffer.at[pl.ds(mine, size), :],
+                sides[group].at[into, pl.ds(0, rows)],
+                turn_sem.at[group, place],
+            )
+            kept.start()
+            turning[which].append(kept.wait)
+            sent = remote(
+                buffer.at[pl.ds(theirs, size), :],
+                sides[group].at[into, pl.ds(rows, rows)],
+                turn_send.at[group, place],
+                turn_recv.at[group, place],
+                other,
+            )
+            sent.start()
+            turning[which].append(sent.wait_send)
+            landing.append(sent)
+
+    def free(which):
+        for wait in turning[which]:
+            wait()
+        turning[which] = []
+
+    def tiles(group, left, emit, start=0, width=None):
+        width = weights[group].shape[1] if width is None else width
+
+        @pl.loop(0, width // 256)
+        def _(at):
+            columns = span(at + start // 256, 256)
+            emit(columns, matmul(left[...], weights[group][:, columns]))
+
+    def stage_norm():
+        norms[...] = line.land()
+        moves.start(norms, norms_out)
+        gain, offset = norms[0:1, :], norms[1:2, :]
+
+        @pl.loop(0, rows // 64)
+        def _(at):
+            block = span(at, 64)
+            values, _ = norm_rows(tokens[block, :].astype(jnp.float32))
+            v.normed[block, :] = (values * gain + offset).astype(jnp.bfloat16)
+
+        share(0, v.normed, 0)
+
+    def stage_head_norm():
+        @pl.loop(0, rows // 64)
+        def _(at):
+            block = span(at, 64)
+            values, _ = norm_rows(head_in[block, :].astype(jnp.float32))
+            v.head_norm[block, :] = values
+
+    def stage_mixed(start, width):
+        def emit(columns, total):
+            v.mixed[:, columns] = total.astype(jnp.bfloat16)
+
+        tiles(0, v.normed, emit, start, width)
+
+    exchange = []
+
+    def stage_swap():
+        exchange.append(swaps.start(v.mixed.at[:, pl.ds(D, 2 * D)], v.far_pair, other))
+        put("mixed")
+
+    def stage_bias():
+        for copy in exchange:
+            copy.wait_recv()
+        fill_bias(bias, far_row, own_row, side)
+        moves.start(bias, bias_out)
+        put("far_pair")
+        free(1)
+
+    def stage_heads(start, stop):
+        @pl.loop(start, stop)
+        def _(at):
+            queries, keys, values = pair_slices(v.mixed, v.far_pair, at)
+            total = None
+            for which in range(2):
+                mask = head_mask(which)
+                weights_now = softmax_columns(keys, queries * mask, bias[...]).astype(jnp.bfloat16)
+                part = matmul_left(values * mask, weights_now)
+                total = part if total is None else total + part
+            low = total.astype(jnp.bfloat16)
+            turned[1][span(at, 2 * HEAD_DIM), :] = low
+            v.attended[:, span(at, 2 * HEAD_DIM)] = low.T
+
+    def stage_proj():
+        share(1, turned[1].at[pl.ds(0, D), :], 1, True)
+
+        def emit(columns, total):
+            v.hidden[:, columns] = tokens[:, columns].astype(jnp.float32) + total
+
+        tiles(1, v.attended, emit)
+        put("hidden")
+        gain, offset = norms[2:3, :], norms[3:4, :]
+
+        @pl.loop(0, rows // 64)
+        def _(at):
+            block = span(at, 64)
+            values, _ = norm_rows(v.hidden[block, :])
+            v.second[block, :] = (values * gain + offset).astype(jnp.bfloat16)
+
+        share(2, v.second, 0)
+
+    def stage_up(start, width):
+        def emit(columns, total):
+            erf = lax.erf(total * 0.5**0.5)
+            half = 0.5 * (1.0 + erf)
+            v.activated[:, columns] = (total * half).astype(jnp.bfloat16)
+            bell = jnp.exp(-0.5 * total * total) * (2.0 * 3.141592653589793) ** -0.5
+            v.slope_inner[:, columns] = (half + total * bell).astype(jnp.bfloat16)
+
+        tiles(2, v.second, emit, start, width)
+
+    def stage_up_end():
+        put("slope_inner")
+        share(3, v.activated, 2)
+
+    def stage_down(start, width):
+        def emit(columns, total):
+            v.block_low[:, columns] = (v.hidden[:, columns] + total).astype(jnp.bfloat16)
+
+        tiles(3, v.activated, emit, start, width)
+
+    def stage_down_end():
+        put("block_low")
+        share(4, v.block_low, 1)
+
+    def stage_cond():
+        def emit(columns, total):
+            gates = jax.nn.sigmoid(total)
+            v.cond_low[:, columns] = (total * gates).astype(jnp.bfloat16)
+            slope = gates * (1.0 + total * (1.0 - gates))
+            v.slope_cond[:, columns] = slope.astype(jnp.bfloat16)
+
+        tiles(4, v.block_low, emit)
+        put("slope_cond")
+        share(5, v.cond_low, 0)
+
+    def stage_mod(start, width):
+        for at in range(start // 256, (start + width) // 256):
+            total = matmul(v.cond_low[...], weights[5][:, at * 256 : (at + 1) * 256])
+            part, block = divmod(at, HW // 256)
+            columns = pl.ds(block * 256, 256)
+            if part == 0:
+                v.shift[:, columns] = total
+            elif part == 1:
+                scale = 1.0 + total
+                v.scale[:, columns] = scale
+                shaped = v.head_norm[:, columns] * scale + v.shift[:, columns]
+                v.shaped[:, columns] = shaped.astype(jnp.bfloat16)
+            else:
+                v.gate[:, columns] = total
+                grad = head_cotangent[:, columns].astype(jnp.float32) * total
+                v.grad_branch[:, columns] = grad.astype(jnp.bfloat16)
+
+    def stage_mod_end():
+        put("scale")
+        put("grad_branch")
+        share(6, v.shaped, 1)
+
+    def stage_inner():
+        def emit(columns, total):
+            gates = jax.nn.sigmoid(total)
+            v.lifted[:, columns] = (total * gates).astype(jnp.bfloat16)
+            slope = gates * (1.0 + total * (1.0 - gates))
+            v.slope_middle[:, columns] = slope.astype(jnp.bfloat16)
+
+        tiles(6, v.shaped, emit)
+        put("slope_middle")
+        share(7, v.lifted, 0)
+
+    def stage_outer():
+        def emit(columns, total):
+            grown = head_in[:, columns].astype(jnp.float32) + v.gate[:, columns] * total
+            v.head_out[:, columns] = grown.astype(jnp.bfloat16)
+            grad = head_cotangent[:, columns].astype(jnp.float32) * total
+            v.grad_gate[:, columns] = grad.astype(jnp.bfloat16)
+
+        tiles(7, v.lifted, emit)
+        put("head_out")
+        put("grad_gate")
+
+    def chunk_tasks(chunk):
+        group, start, width = chunks[chunk]
+        final = start + width == weights[group].shape[1]
+        if group == 0:
+            tasks = [lambda: stage_mixed(start, width)]
+            if final:
+                tasks += [stage_swap, stage_bias]
+                tasks += [functools.partial(stage_heads, at, at + 2) for at in range(0, 6, 2)]
+        elif group == 1:
+            tasks = [stage_proj]
+        elif group == 2:
+            tasks = [lambda: stage_up(start, width)]
+            if final:
+                tasks.append(stage_up_end)
+        elif group == 3:
+            tasks = [lambda: stage_down(start, width)]
+            if final:
+                tasks.append(stage_down_end)
+        elif group == 4:
+            tasks = [stage_cond]
+        elif group == 5:
+            tasks = [lambda: stage_mod(start, width)]
+            if final:
+                tasks.append(stage_mod_end)
+        elif group == 6:
+            tasks = [stage_inner]
+        else:
+            tasks = [stage_outer]
+        return [(chunk, task) for task in tasks]
+
+    total = len(chunks)
+    line.launch(spread)
+    exchange.append(swaps.start(own_row, far_row, other))
+    queue = [item for chunk in range(total) for item in chunk_tasks(chunk)]
+    for step in range(-AHEAD_SEQ, total + 3):
+        if step + AHEAD_SEQ < total:
+            group, start, _ = chunks[step + AHEAD_SEQ]
+            if start == 0:
+                flow.cast(group)
+            flow.first(step + AHEAD_SEQ)
+        if 0 <= step + AHEAD_DP < total:
+            flow.second(step + AHEAD_DP)
+        if 0 <= step - 1 < total:
+            flow.third(step - 1)
+        if step == -2:
+            stage_head_norm()
+        if step == -1:
+            line.launch(line.land())
+        if step == 0:
+            stage_norm()
+        done = 0
+        while queue and queue[0][0] <= step - 3 and (done < TASKS or step >= total):
+            chunk, task = queue.pop(0)
+            if chunk in loading:
+                loading.pop(chunk).wait()
+            task()
+            done += 1
+        if 0 <= step - 2 < total:
+            flow.fourth(step - 2)
+            flow.fifth(step - 2)
+            load(step - 2)
+    flow.finish()
+    moves.finish()
+    swaps.finish()
+    for which in range(3):
+        free(which)
+    for copy in landing:
+        copy.wait_recv()
+
+
+def forward_all(masters, tokens, head_in, head_cotangent, image_ids, norm_params):
+    devices = lax.axis_size("dp") * lax.axis_size("side") * lax.axis_size("seq")
+    count = lax.axis_size("seq")
+    chunks = chunk_list([master.shape for master in masters])
+    total = len(chunks)
+    rows = tokens.shape[0]
+    low, full = jnp.bfloat16, jnp.float32
+    fulls = [jax.ShapeDtypeStruct((devices * m.shape[0], m.shape[1]), low) for m in masters]
+    sides = [jax.ShapeDtypeStruct((devices * m.shape[0] // 2, 2 * rows), low) for m in masters]
+    outs = [jax.ShapeDtypeStruct((rows, width), kind) for _, width, kind in FORWARD_OUT]
+    extra = [jax.ShapeDtypeStruct((2 * rows, rows), full), jax.ShapeDtypeStruct((8, D), full)]
+    scratch = [pltpu.VMEM(item.shape, low) for item in fulls]
+    scratch += [pltpu.VMEM((rows, width), kind) for _, width, kind in FORWARD_OUT + FORWARD_LOCAL]
+    scratch += [
+        pltpu.VMEM((2 * rows, rows), full),
+        pltpu.VMEM((8, rows), full),
+        pltpu.VMEM((8, rows), full),
+        pltpu.VMEM((count + 8, 8, D), full),
+        pltpu.VMEM((8, D), full),
+        pltpu.VMEM((HW, rows), low),
+        pltpu.VMEM((HW, rows), low),
+        pltpu.VMEM((4 * D, rows), low),
+    ]
+    for master in masters:
+        depth, width = master.shape
+        if depth % 16 == 0:
+            scratch.append(pltpu.VMEM((depth, width), low))
+        else:
+            scratch.append(pltpu.VMEM((count, depth, width), low))
+            scratch.append(pltpu.VMEM((count * depth, width), low))
+    dma = pltpu.SemaphoreType.DMA
+    scratch += [
+        dma((total, count + 7)),
+        dma((total, count + 7)),
+        dma((total,)),
+        dma((total,)),
+        dma((16,)),
+        dma((8 + count,)),
+        dma((8 + count,)),
+        dma((8, 4)),
+        dma((8, 4)),
+        dma((8, 4)),
+    ]
+    vmem, hbm = pl.BlockSpec(memory_space=pltpu.VMEM), pl.BlockSpec(memory_space=pltpu.HBM)
+    results = pl.pallas_call(
+        lambda *refs: forward_kernel(chunks, count, *refs),
+        out_shape=fulls + sides + outs + extra,
+        in_specs=[vmem] * 13,
+        out_specs=[hbm] * (16 + len(outs) + 2),
+        scratch_shapes=scratch,
+        compiler_params=pltpu.CompilerParams(
+            collective_id=0, has_side_effects=True, vmem_limit_bytes=63 * 2**20
+        ),
+        name="forward",
+    )(*masters, tokens, head_in, head_cotangent, image_ids[None, :], norm_params.T)
+    named = dict(zip([name for name, _, _ in FORWARD_OUT], results[16:]))
+    named["bias"], named["norms"] = results[-2:]
+    return results[:8], results[8:16], named
+
+
+class Scatter:
+    def __init__(self, chunks, parts, inbox, after, slabs, pieces, finals, squares, sends, recvs):
+        self.chunks, self.parts, self.inbox, self.after = chunks, parts, inbox, after
+        self.slabs, self.pieces, self.finals, self.squares = slabs, pieces, finals, squares
+        self.sends, self.recvs = sends, recvs
+        self.dp, self.side, self.seq, near, far, self.along, _ = places()
+        self.near, self.far = (near, self.side, self.seq), (far, self.side, self.seq)
+        self.count = len(self.along) + 1
+        self.started = []
+        self.coming = {}
+
+    def send(self, chunk, which, source, target, peer):
+        copy = remote(source, target, self.sends.at[chunk, which], self.recvs.at[chunk, which], peer)
+        copy.start()
+        self.started.append(copy)
+        self.coming[chunk, which] = copy
+
+    def land(self, chunk, *which):
+        for item in which:
+            self.coming.pop((chunk, item)).wait_recv()
+
+    def shape(self, chunk):
+        group, start, width = self.chunks[chunk]
+        size = self.parts[group].shape[1]
+        return group, start, width, size, size // 2
+
+    def first(self, chunk):
+        group, start, width, size, half = self.shape(chunk)
+        columns, part, inbox = pl.ds(start, width), self.parts[group], self.inbox[group]
+        upper, lower = pl.ds(0, half), pl.ds(half, half)
+        for item, block in enumerate((1, 3)):
+            self.send(chunk, item, part.at[block, upper, columns], inbox.at[item, :, columns], self.near)
+        for item, block in enumerate((2, 3)):
+            self.send(
+                chunk, 2 + item, part.at[block, lower, columns], inbox.at[2 + item, :, columns], self.far
+            )
+
+    def tiles(self, chunk, work):
+        _, start, width, _, _ = self.shape(chunk)
+
+        @pl.loop(0, width // 256)
+        def _(at):
+            work(pl.ds(pl.multiple_of(start + at * 256, 256), 256))
+
+    def second(self, chunk):
+        group, start, width, size, half = self.shape(chunk)
+        columns, part, inbox = pl.ds(start, width), self.parts[group], self.inbox[group]
+        upper, lower = pl.ds(0, half), pl.ds(half, half)
+        self.land(chunk, 0, 1, 2, 3)
+
+        def work(span_now):
+            for block, rows, item in ((2, upper, 1), (1, lower, 3)):
+                total = part[block, rows, span_now].astype(jnp.float32)
+                total = total + inbox[item, :, span_now].astype(jnp.float32)
+                part[block, rows, span_now] = total.astype(jnp.bfloat16)
+
+        self.tiles(chunk, work)
+        after = self.after[group]
+        self.send(chunk, 4, part.at[1, lower, columns], after.at[0, :, columns], self.near)
+        self.send(chunk, 5, part.at[2, upper, columns], after.at[1, :, columns], self.far)
+
+    def third(self, chunk):
+        group, start, width, size, half = self.shape(chunk)
+        columns, part, inbox = pl.ds(start, width), self.parts[group], self.inbox[group]
+        upper, lower = pl.ds(0, half), pl.ds(half, half)
+        after = self.after[group]
+        self.land(chunk, 4, 5)
+        slab = self.slabs[group]
+        depth = size // self.count
+
+        def work(span_now):
+            for rows, item, last, base in ((upper, 0, 1, 0), (lower, 2, 0, self.count // 2)):
+                total = part[0, rows, span_now].astype(jnp.float32)
+                total = total + inbox[item, :, span_now].astype(jnp.float32)
+                total = total + after[last, :, span_now].astype(jnp.float32)
+                for place in range(self.count // 2):
+                    piece = total[place * depth : (place + 1) * depth].astype(jnp.bfloat16)
+                    slab[base + place, :, span_now] = piece
+
+        self.tiles(chunk, work)
+        for step, peer in enumerate(self.along):
+            self.send(
+                chunk,
+                6 + step,
+                slab.at[peer, :, columns],
+                self.pieces[group].at[step, :, columns],
+                (self.dp, self.side, peer),
+            )
+
+    def fourth(self, chunk):
+        group, start, width, size, half = self.shape(chunk)
+        self.land(chunk, *(6 + step for step in range(self.count - 1)))
+        slab, pieces, final = self.slabs[group], self.pieces[group], self.finals[group]
+
+        def work(span_now):
+            total = slab[self.seq, :, span_now].astype(jnp.float32)
+            for step in range(self.count - 1):
+                total = total + pieces[step, :, span_now].astype(jnp.float32)
+            final[:, span_now] = total
+            self.squares[0:1, :] += jnp.sum(total * total, axis=0, keepdims=True)
+
+        self.tiles(chunk, work)
+
+    def finish(self):
+        for copy in self.started:
+            copy.wait_send()
+
+
+LAG = 1
+
+
+BACKWARD_IN = (
+    "grad_branch",
+    "slope_middle",
+    "head_in",
+    "head_cotangent",
+    "scale",
+    "grad_gate",
+    "slope_cond",
+    "out_cotangent",
+    "slope_inner",
+    "hidden",
+    "norms",
+    "mixed",
+    "far_pair",
+    "bias",
+    "tokens",
+)
+
+
+def norm_back(grads, values, scale):
+    first = jnp.mean(grads, axis=-1, keepdims=True)
+    second = jnp.mean(grads * values, axis=-1, keepdims=True)
+    return scale * (grads - first - values * second)
+
+
+def backward_kernel(chunks, count, *refs):
+    rest = list(refs)
+
+    def take(number):
+        taken = rest[:number]
+        del rest[:number]
+        return taken
+
+    weights, sides = take(8), take(8)
+    given = dict(zip(BACKWARD_IN, take(len(BACKWARD_IN))))
+    finals = take(8)
+    head_in_grad, tokens_grad, norm_grads, norm_out = take(4)
+    grads, parts, inbox, after, slabs, pieces = (take(8) for _ in range(6))
+    small, large, tile_box = take(3)
+    into = {
+        "grad_branch": grads[7].at[pl.ds(0, grads[7].shape[0] // 2), :],
+        "slope_middle": grads[6].at[pl.ds(0, grads[6].shape[0] // 2), :],
+        "grad_gate": grads[5].at[pl.ds(0, grads[5].shape[0] // 2), pl.ds(2 * HW, HW)],
+        "slope_cond": grads[4].at[pl.ds(0, grads[4].shape[0] // 2), :],
+        "slope_inner": grads[2].at[pl.ds(0, grads[2].shape[0] // 2), :],
+    }
+    held = [name for name in BACKWARD_IN if name not in into]
+    local = SimpleNamespace(**dict(zip(held, take(10))))
+    spare, block_grad, attended_grad, back_pair, squares, box, square_box = take(7)
+    sends, recvs, load_sem, side_sem, tile_sem, swap_send, swap_recv = rest
+
+    dp, side, seq, near, far, along, _ = places()
+    other = (dp, 1 - side, seq)
+    greet(all_peers())
+    rows = local.tokens.shape[0]
+    own, pair = pl.ds(0, rows), pl.ds(rows, rows)
+    swaps = Swaps(swap_send, swap_recv)
+    flow = Scatter(chunks, parts, inbox, after, slabs, pieces, finals, squares, sends, recvs)
+    loading = {}
+    for item, name in enumerate(BACKWARD_IN):
+        target = into[name] if name in into else getattr(local, name)
+        loading[name] = pltpu.make_async_copy(given[name], target, load_sem.at[item])
+    order = [group for group in range(7, -1, -1)]
+    slim = [group for group in order if sides[group].shape[0] <= small.shape[1]]
+    side_slot = {}
+    side_copy = {}
+
+    def side_load(group):
+        depth = sides[group].shape[0]
+        if group in slim:
+            target = small.at[slim.index(group) % 2, pl.ds(0, depth), :]
+        else:
+            target = large
+        side_slot[group] = target
+        side_copy[group] = pltpu.make_async_copy(sides[group], target, side_sem.at[group])
+        side_copy[group].start()
+
+    def ready(*names):
+        for name in names:
+            loading.pop(name).wait()
+
+    tile_list = [
+        (group, at) for group in order for at in range(weights[group].shape[0] // 256)
+    ]
+    tile_copy = {}
+    depth_box = tile_box.shape[0]
+
+    def tile_load(item):
+        if item >= len(tile_list):
+            return
+        group, at = tile_list[item]
+        copy = pltpu.make_async_copy(
+            weights[group].at[pl.ds(at * 256, 256), :],
+            tile_box.at[item % depth_box, :, pl.ds(0, weights[group].shape[1])],
+            tile_sem.at[item],
+        )
+        tile_copy[item] = copy
+        copy.start()
+
+    loading["grad_branch"].start()
+    for item in range(depth_box):
+        tile_load(item)
+    loading["slope_middle"].start()
+    side_load(slim[0])
+    side_load(slim[1])
+    for name in BACKWARD_IN[2:]:
+        loading[name].start()
+    for group in order:
+        if group not in slim:
+            side_load(group)
+    squares[...] = jnp.zeros_like(squares)
+    norm_grads[...] = jnp.zeros_like(norm_grads)
+    at_tile = [0]
+
+    def back(group, emit):
+        width = weights[group].shape[1]
+        for at in range(weights[group].shape[0] // 256):
+            item = at_tile[0]
+            at_tile[0] += 1
+            tile_copy.pop(item).wait()
+            total = matmul_right(
+                grads[group][own, :], tile_box[item % depth_box, :, pl.ds(0, width)]
+            )
+            emit(pl.ds(at * 256, 256), total)
+            tile_load(item + depth_box)
+
+    coming = {}
+
+    def share(group):
+        coming[group] = swaps.start(grads[group].at[own, :], grads[group].at[pair, :], other)
+
+    def product(chunk):
+        group, start, width = chunks[chunk]
+        if group in coming:
+            coming.pop(group).wait_recv()
+            side_copy.pop(group).wait()
+        left, part = side_slot[group], parts[group]
+        size = part.shape[1]
+        whole = group in slim
+
+        @pl.loop(0, width // 256)
+        def _(at):
+            columns = pl.ds(pl.multiple_of(start + at * 256, 256), 256)
+            right = grads[group][:, columns]
+            if whole:
+                total = matmul(left[...], right).astype(jnp.bfloat16)
+                for block in range(4):
+                    part[block, :, columns] = total[block * size : (block + 1) * size]
+            else:
+                for block in range(4):
+                    total = matmul(left[pl.ds(block * size, size), :], right)
+                    part[block, :, columns] = total.astype(jnp.bfloat16)
+
+        if start + width == weights[group].shape[1]:
+            if group in slim and slim.index(group) + 2 < len(slim):
+                side_load(slim[slim.index(group) + 2])
+
+    def step(chunk):
+        total = len(chunks)
+        if chunk < total:
+            product(chunk)
+            flow.first(chunk)
+        if 0 <= chunk - LAG < total:
+            flow.second(chunk - LAG)
+        if 0 <= chunk - LAG - 1 < total:
+            flow.third(chunk - LAG - 1)
+        if 0 <= chunk - LAG - 2 < total:
+            flow.fourth(chunk - LAG - 2)
+
+    def stage_outer():
+        ready("grad_branch")
+        share(7)
+        ready("slope_middle")
+
+        def emit(columns, total):
+            slope = grads[6][own, columns].astype(jnp.float32)
+            grads[6][own, columns] = (total * slope).astype(jnp.bfloat16)
+
+        back(7, emit)
+        share(6)
+
+    def stage_inner():
+        def emit(columns, total):
+            spare[:, columns] = total
+
+        back(6, emit)
+        ready("head_in", "head_cotangent", "scale", "grad_gate")
+
+        @pl.loop(0, rows // 32)
+        def _(at):
+            block = span(at, 32)
+            values, scale = norm_rows(local.head_in[block, :].astype(jnp.float32))
+            grad = spare[block, pl.ds(0, HW)]
+            grads[5][block, pl.ds(0, HW)] = grad.astype(jnp.bfloat16)
+            grads[5][block, pl.ds(HW, HW)] = (grad * values).astype(jnp.bfloat16)
+            passed = norm_back(grad * local.scale[block, :], values, scale)
+            head_in_grad[block, :] = local.head_cotangent[block, :].astype(jnp.float32) + passed
+
+        share(5)
+
+    def stage_mod():
+        ready("slope_cond")
+
+        def emit(columns, total):
+            slope = grads[4][own, columns].astype(jnp.float32)
+            grads[4][own, columns] = (total * slope).astype(jnp.bfloat16)
+
+        back(5, emit)
+        share(4)
+
+    def stage_cond():
+        ready("out_cotangent")
+
+        def emit(columns, total):
+            grad = local.out_cotangent[:, columns].astype(jnp.float32) + total
+            block_grad[:, columns] = grad
+            grads[3][own, columns] = grad.astype(jnp.bfloat16)
+
+        back(4, emit)
+        share(3)
+
+    def stage_down():
+        ready("slope_inner")
+
+        def emit(columns, total):
+            slope = grads[2][own, columns].astype(jnp.float32)
+            grads[2][own, columns] = (total * slope).astype(jnp.bfloat16)
+
+        back(3, emit)
+        share(2)
+
+    def norm_stage(source, base, emit):
+        gain = local.norms[base : base + 1, :]
+
+        @pl.loop(0, rows // 32)
+        def _(at):
+            block = span(at, 32)
+            values, scale = norm_rows(source[block, :].astype(jnp.float32))
+            grad = spare[block, pl.ds(0, D)]
+            norm_grads[base : base + 1, :] += jnp.sum(grad * values, axis=0, keepdims=True)
+            norm_grads[base + 1 : base + 2, :] += jnp.sum(grad, axis=0, keepdims=True)
+            emit(block, norm_back(grad * gain, values, scale))
+
+    def stage_up():
+        def keep(columns, total):
+            spare[:, columns] = total
+
+        back(2, keep)
+        ready("hidden", "norms")
+
+        def emit(block, passed):
+            grad = block_grad[block, :] + passed
+            tokens_grad[block, :] = grad
+            grads[1][block, :] = grad.astype(jnp.bfloat16)
+
+        norm_stage(local.hidden, 2, emit)
+        share(1)
+
+    def stage_proj():
+        def emit(columns, total):
+            attended_grad[:, columns] = total.astype(jnp.bfloat16)
+
+        back(1, emit)
+        ready("mixed", "far_pair", "bias")
+
+    def stage_heads(start, stop):
+        width = 2 * HEAD_DIM
+        scaling = HEAD_DIM ** (-0.5)
+
+        @pl.loop(start, stop)
+        def _(at):
+            queries, keys, values = pair_slices(local.mixed, local.far_pair, at)
+            outer = attended_grad[:, span(at, width)]
+            query_part = key_part = value_part = None
+            for which in range(2):
+                mask = head_mask(which)
+                query_now, outer_now = queries * mask, outer * mask
+                chances = softmax_columns(keys, query_now, local.bias[...])
+                slopes = matmul_right(values, outer_now)
+                inner = jnp.sum(chances * slopes, axis=0, keepdims=True)
+                score_grad = (chances * (slopes - inner)).astype(jnp.bfloat16)
+                value_now = matmul(chances.astype(jnp.bfloat16), outer_now)
+                key_now = matmul(score_grad, query_now)
+                query_side = matmul_left(keys * mask, score_grad)
+                if which == 0:
+                    query_part, key_part, value_part = query_side, key_now, value_now
+                else:
+                    query_part = query_part + query_side
+                    key_part = key_part + key_now
+                    value_part = value_part + value_now
+            grads[0][own, span(at, width)] = (query_part * scaling).astype(jnp.bfloat16).T
+            key_part = key_part * scaling
+            first, second = span(at, width), span(at + D // width, width)
+            local.far_pair[:, first] = key_part[:rows].astype(jnp.bfloat16)
+            local.far_pair[:, second] = value_part[:rows].astype(jnp.bfloat16)
+            spare[:, first] = key_part[rows:]
+            spare[:, second] = value_part[rows:]
+
+    def stage_return():
+        coming["back"] = swaps.start(local.far_pair, back_pair, other)
+
+    def stage_merge():
+        coming.pop("back").wait_recv()
+
+        @pl.loop(0, 2 * D // 256)
+        def _(at):
+            columns = span(at, 256)
+            total = spare[:, columns] + back_pair[:, columns].astype(jnp.float32)
+            grads[0][own, span(at + D // 256, 256)] = total.astype(jnp.bfloat16)
+
+        share(0)
+
+    def stage_attend():
+        def keep(columns, total):
+            spare[:, columns] = total
+
+        back(0, keep)
+        ready("tokens")
+
+        def emit(block, passed):
+            tokens_grad[block, :] = tokens_grad[block, :] + passed
+
+        norm_stage(local.tokens, 0, emit)
+
+    stage_outer()
+    stages = [
+        stage_inner,
+        stage_mod,
+        stage_cond,
+        stage_down,
+        stage_up,
+        stage_proj,
+        lambda: stage_heads(0, 2),
+        lambda: stage_heads(2, 4),
+        lambda: stage_heads(4, 6),
+        stage_return,
+        stage_merge,
+        stage_attend,
+    ]
+    line = LineSum(box, swaps)
+    total = len(chunks)
+    for chunk in range(total + LAG + 3):
+        group = chunks[min(chunk, total - 1)][0]
+        needed = {7: 0, 6: 0, 5: 1, 4: 2, 3: 3, 2: 4, 1: 5, 0: 11}[group]
+        while stages and 12 - len(stages) < needed:
+            stages.pop(0)()
+        step(chunk)
+        if stages:
+            stages.pop(0)()
+            if not stages:
+                line.launch(norm_grads[...])
+        elif line.level == 0:
+            line.launch(line.land())
+        elif line.level == 1:
+            sums = line.land()
+            norm_grads[...] = sums
+    last = LineSum(square_box, swaps)
+    last.launch(squares[...])
+    last.launch(last.land())
+    sums = norm_grads[...]
+    flat = jnp.sum(last.land(), axis=0, keepdims=True)
+    whole = jnp.sum(flat, axis=1, keepdims=True)
+    extra = jnp.sum(jnp.sum(sums * sums, axis=0, keepdims=True), axis=1, keepdims=True)
+    norm_out[...] = jnp.broadcast_to(jnp.sqrt(whole + extra), norm_out.shape)
+    flow.finish()
+    swaps.finish()
+
+
+def backward_chunks(masters):
+    chunks = chunk_list(masters)
+    chunks = [item for group in range(7, -1, -1) for item in chunks if item[0] == group]
+    group, start, width = chunks.pop()
+    for size in (width - width // 2 // 256 * 256, width // 2 // 256 * 256):
+        chunks.append((group, start, size)) if size else None
+        start += size
+    return chunks
+
+
+def backward_all(masters, weights, sides, named):
+    count = lax.axis_size("seq")
+    shapes = [master.shape for master in masters]
+    chunks = backward_chunks(shapes)
+    total = len(chunks)
+    rows = named["tokens"].shape[0]
+    low, full = jnp.bfloat16, jnp.float32
+    vmem, hbm = pl.BlockSpec(memory_space=pltpu.VMEM), pl.BlockSpec(memory_space=pltpu.HBM)
+    given = [named[name] for name in BACKWARD_IN]
+    outs = [jax.ShapeDtypeStruct(shape, full) for shape in shapes]
+    outs += [
+        jax.ShapeDtypeStruct((rows, HW), full),
+        jax.ShapeDtypeStruct((rows, D), full),
+        jax.ShapeDtypeStruct((8, D), full),
+        jax.ShapeDtypeStruct((8, 128), full),
+    ]
+    scratch = [pltpu.VMEM((2 * rows, width), low) for _, width in shapes]
+    scratch += [pltpu.VMEM((4, count * depth, width), low) for depth, width in shapes]
+    scratch += [pltpu.VMEM((4, count * depth // 2, width), low) for depth, width in shapes]
+    scratch += [pltpu.VMEM((2, count * depth // 2, width), low) for depth, width in shapes]
+    scratch += [pltpu.VMEM((count, depth, width), low) for depth, width in shapes]
+    scratch += [pltpu.VMEM((count - 1, depth, width), low) for depth, width in shapes]
+    scratch += [
+        pltpu.VMEM((2, HW // 2, 2 * rows), low),
+        pltpu.VMEM((2 * D, 2 * rows), low),
+        pltpu.VMEM((3, 256, 3 * HW), low),
+        pltpu.VMEM((rows, HW), low),
+        pltpu.VMEM((rows, HW), low),
+        pltpu.VMEM((rows, HW), full),
+        pltpu.VMEM((rows, D), low),
+        pltpu.VMEM((rows, D), full),
+        pltpu.VMEM((8, D), full),
+        pltpu.VMEM((rows, 3 * D), low),
+        pltpu.VMEM((rows, 2 * D), low),
+        pltpu.VMEM((2 * rows, rows), full),
+        pltpu.VMEM((rows, D), low),
+        pltpu.VMEM((rows, 2 * D), full),
+        pltpu.VMEM((rows, D), full),
+        pltpu.VMEM((rows, D), low),
+        pltpu.VMEM((rows, 2 * D), low),
+        pltpu.VMEM((8, 256), full),
+        pltpu.VMEM((count + 8, 8, D), full),
+        pltpu.VMEM((count + 8, 8, 256), full),
+    ]
+    dma = pltpu.SemaphoreType.DMA
+    scratch += [
+        dma((total, 5 + count)),
+        dma((total, 5 + count)),
+        dma((len(BACKWARD_IN),)),
+        dma((8,)),
+        dma((sum(w.shape[0] // 256 for w in weights),)),
+        dma((21 + 2 * count,)),
+        dma((21 + 2 * count,)),
+    ]
+    return pl.pallas_call(
+        lambda *refs: backward_kernel(chunks, count, *refs),
+        out_shape=outs,
+        in_specs=[hbm] * (16 + len(given)),
+        out_specs=[vmem] * len(outs),
+        scratch_shapes=scratch,
+        compiler_params=pltpu.CompilerParams(
+            collective_id=1, has_side_effects=True, vmem_limit_bytes=64 * 2**20
+        ),
+        name="backward",
+    )(*weights, *sides, *given)
+
+
+def optimizer_kernel(*refs):
+    rest = list(refs)
+
+    def take(number):
+        taken = rest[:number]
+        del rest[:number]
+        return taken
+
+    given = [take(5) for _ in range(8)]
+    passed = take(4)
+    small, grad_norm = take(5), rest.pop(0)
+    results = [take(4) for _ in range(8)]
+    kept = take(4)
+    small_results = take(4)
+    held = [take(5) for _ in range(8)]
+    made = [take(4) for _ in range(8)]
+    carried = take(4)
+    load_sem, save_sem, pass_sem = rest
+    loads, saves = [], []
+    for group in range(8):
+        for item in range(5):
+            copy = pltpu.make_async_copy(
+                given[group][item], held[group][item], load_sem.at[group, item]
+            )
+            copy.start()
+            loads.append(copy)
+    for item in range(4):
+        pltpu.make_async_copy(passed[item], carried[item], pass_sem.at[0, item]).start()
+    factor = jnp.minimum(1.0, clip_limit / (grad_norm[0:1, 0:1] + 1e-06))
+    keep_old, take_new = average_factors()
+
+    def update(source, target, columns, decays, rate):
+        gradient, master, moment, square, average = (ref[:, columns] for ref in source)
+        put(gradient, master, moment, square, average, target, columns, decays, rate)
+
+    def put(gradient, master, moment, square, average, target, columns, decays, rate):
+        fresh = adam_step(master, gradient * factor, moment, square, decays, rate)
+        for item in range(3):
+            target[item][:, columns] = fresh[item]
+        target[3][:, columns] = keep_old * average + take_new * fresh[0]
+
+    width = small[1].shape[1]
+    total = small[0].shape[1]
+    place = (lax.axis_index("dp") * 2 + lax.axis_index("side")) * lax.axis_size(
+        "seq"
+    ) + lax.axis_index("seq")
+    turned = pltpu.roll(small[0][...], lax.rem(total - place * width, total), 1)
+    own = [turned[0:4, 0:width]] + [ref[...] for ref in small[1:]]
+    put(*own, small_results, slice(None), 0.0, learn_rates[8])
+    for group in range(8):
+        for item in range(5):
+            loads[group * 5 + item].wait()
+
+        @pl.loop(0, held[group][0].shape[1] // 256)
+        def _(at):
+            columns = pl.ds(pl.multiple_of(at * 256, 256), 256)
+            update(held[group], made[group], columns, 1.0, learn_rates[group])
+
+        for item in range(4):
+            copy = pltpu.make_async_copy(
+                made[group][item], results[group][item], save_sem.at[group, item]
+            )
+            copy.start()
+            saves.append(copy)
+        if group % 2:
+            item = group // 2
+            pltpu.make_async_copy(passed[item], carried[item], pass_sem.at[0, item]).wait()
+            copy = pltpu.make_async_copy(carried[item], kept[item], pass_sem.at[1, item])
+            copy.start()
+            saves.append(copy)
+    for copy in saves:
+        copy.wait()
+
+
+def optimizer_all(gradients, passed, norm_grads, grad_norm, masters, moments, squares, averages):
+    full = jnp.float32
+    vmem, hbm = pl.BlockSpec(memory_space=pltpu.VMEM), pl.BlockSpec(memory_space=pltpu.HBM)
+    given = []
+    for group in range(8):
+        given += [
+            gradients[group],
+            masters[group],
+            moments[group],
+            squares[group],
+            averages[group],
+        ]
+    small = [masters[8].T, moments[8].T, squares[8].T, averages[8].T]
+    given += [*passed, norm_grads, *small, grad_norm]
+    shapes = [master.shape for master in masters[:8]]
+    outs = [jax.ShapeDtypeStruct(shape, full) for shape in shapes for _ in range(4)]
+    outs += [jax.ShapeDtypeStruct(item.shape, item.dtype) for item in passed]
+    outs += [jax.ShapeDtypeStruct(small[0].shape, full) for _ in range(4)]
+    scratch = [pltpu.VMEM(shape, full) for shape in shapes for _ in range(5)]
+    scratch += [pltpu.VMEM(shape, full) for shape in shapes for _ in range(4)]
+    scratch += [pltpu.VMEM(item.shape, item.dtype) for item in passed]
+    dma = pltpu.SemaphoreType.DMA
+    scratch += [dma((8, 5)), dma((8, 4)), dma((2, 4))]
+    results = pl.pallas_call(
+        optimizer_kernel,
+        out_shape=outs,
+        in_specs=[hbm] * 44 + [vmem] * 6,
+        out_specs=[hbm] * 36 + [vmem] * 4,
+        scratch_shapes=scratch,
+        compiler_params=pltpu.CompilerParams(vmem_limit_bytes=63 * 2**20),
+        name="optimizer",
+    )(*given)
+    fresh = [results[4 * group : 4 * group + 4] for group in range(8)]
+    return results[32:36], fresh + [[item.T for item in results[36:]]]
+
+
+def body(*arrays):
+    tokens, head_in, image_ids, out_cotangent, head_cotangent = arrays[:5]
+    masters, moments, squares, averages = (arrays[at : at + 9] for at in (5, 14, 23, 32))
+    sides = lax.axis_size("dp") == 4 and lax.axis_size("side") == 2
+    if not sides or masters[0].shape[0] % 8 or lax.axis_size("seq") % 2:
+        return plain_body(*arrays)
+    weights, turned, named = forward_all(
+        masters[:8], tokens, head_in, head_cotangent, image_ids, masters[8]
+    )
+    named = dict(
+        named,
+        tokens=tokens,
+        head_in=head_in,
+        head_cotangent=head_cotangent,
+        out_cotangent=out_cotangent,
+    )
+    results = backward_all(masters[:8], weights, turned, named)
+    gradients = results[:8]
+    head_in_grad, tokens_grad, norm_grads, grad_norm = results[8:]
+    passed = [named["block_low"], named["head_out"], tokens_grad, head_in_grad]
+    passed, fresh = optimizer_all(
+        gradients, passed, norm_grads, grad_norm, masters, moments, squares, averages
+    )
+    return (
+        (*passed, grad_norm[0, 0])
+        + tuple(item for group in fresh for item in group[:3])
+        + tuple(group[3] for group in fresh)
+    )
+
+
+def plain_body(
     tokens,
     head_in,
     image_ids,
@@ -399,25 +1571,26 @@
     ema_outer,
     ema_norms,
 ):
-    masters = (
-        weight_attend,
-        weight_proj,
-        weight_up,
-        weight_down,
-        weight_cond,
-        weight_mod,
-        weight_inner,
-        weight_outer,
+    used = (
+        lax.all_gather(
+            weight_attend.astype(jnp.bfloat16), AXES, axis=0, tiled=True
+        ),
+        lax.all_gather(weight_proj.astype(jnp.bfloat16), AXES, axis=0, tiled=True),
+        lax.all_gather(weight_up.astype(jnp.bfloat16), AXES, axis=0, tiled=True),
+        lax.all_gather(weight_down.astype(jnp.bfloat16), AXES, axis=0, tiled=True),
+        lax.all_gather(weight_cond.astype(jnp.bfloat16), AXES, axis=0, tiled=True),
+        lax.all_gather(weight_mod.astype(jnp.bfloat16), AXES, axis=0, tiled=True),
+        lax.all_gather(
+            weight_inner.astype(jnp.bfloat16), AXES, axis=0, tiled=True
+        ),
+        lax.all_gather(
+            weight_outer.astype(jnp.bfloat16), AXES, axis=0, tiled=True
+        ),
+        lax.all_gather(norm_params.astype(jnp.bfloat16), AXES, axis=0, tiled=True),
     )
-    if lax.axis_size("dp") == 4 and lax.axis_size("side") == 2 and weight_attend.shape[0] % 8 == 0:
-        gathered = gather_all(masters)
-    else:
-        gathered = [
-            lax.all_gather(master.astype(jnp.bfloat16), AXES, axis=0, tiled=True)
-            for master in masters
-        ]
-    use_attend, use_proj, use_up, use_down, use_cond, use_mod, use_inner, use_outer = gathered
-    use_norms = lax.all_gather(norm_params.astype(jnp.bfloat16), AXES, axis=0, tiled=True)
+    use_attend, use_proj, use_up, use_down, use_cond, use_mod, use_inner, use_outer, use_norms = (
+        used
+    )
     norm_set = use_norms.astype(jnp.float32)
     inputs = tokens.astype(jnp.float32)
     row_count = tokens.shape[0]
@@ -529,18 +1702,18 @@
     tokens_grad = grad_hidden + tokens_part
     grad_norms = jnp.stack([grad_gain_one, grad_bias_one, grad_gain_two, grad_bias_two], axis=1)
     owned = (
-        lax.psum_scatter(grad_attend, ("dp", "side", "seq"), scatter_dimension=0, tiled=True),
-        lax.psum_scatter(grad_proj, ("dp", "side", "seq"), scatter_dimension=0, tiled=True),
-        lax.psum_scatter(grad_up, ("dp", "side", "seq"), scatter_dimension=0, tiled=True),
-        lax.psum_scatter(grad_down, ("dp", "side", "seq"), scatter_dimension=0, tiled=True),
-        lax.psum_scatter(grad_cond, ("dp", "side", "seq"), scatter_dimension=0, tiled=True),
-        lax.psum_scatter(grad_mod, ("dp", "side", "seq"), scatter_dimension=0, tiled=True),
-        lax.psum_scatter(grad_inner, ("dp", "side", "seq"), scatter_dimension=0, tiled=True),
-        lax.psum_scatter(grad_outer, ("dp", "side", "seq"), scatter_dimension=0, tiled=True),
-        lax.psum_scatter(grad_norms, ("dp", "side", "seq"), scatter_dimension=0, tiled=True),
+        lax.psum_scatter(grad_attend, AXES, scatter_dimension=0, tiled=True),
+        lax.psum_scatter(grad_proj, AXES, scatter_dimension=0, tiled=True),
+        lax.psum_scatter(grad_up, AXES, scatter_dimension=0, tiled=True),
+        lax.psum_scatter(grad_down, AXES, scatter_dimension=0, tiled=True),
+        lax.psum_scatter(grad_cond, AXES, scatter_dimension=0, tiled=True),
+        lax.psum_scatter(grad_mod, AXES, scatter_dimension=0, tiled=True),
+        lax.psum_scatter(grad_inner, AXES, scatter_dimension=0, tiled=True),
+        lax.psum_scatter(grad_outer, AXES, scatter_dimension=0, tiled=True),
+        lax.psum_scatter(grad_norms, AXES, scatter_dimension=0, tiled=True),
     )
     local_squares = sum((jnp.sum(gradient * gradient) for gradient in owned))
-    grad_norm = jnp.sqrt(lax.psum(local_squares, ("dp", "side", "seq")))
+    grad_norm = jnp.sqrt(lax.psum(local_squares, AXES))
     factor = jnp.minimum(1.0, clip_limit / (grad_norm + 1e-06))
     masters = [
         weight_attend,
@@ -609,90 +1782,7 @@
 
 
 def solution(mesh):
-    in_specs = (
-        P(("dp", "side", "seq"), None),
-        P(("dp", "side", "seq"), None),
-        P(("dp", "side", "seq")),
-        P(("dp", "side", "seq"), None),
-        P(("dp", "side", "seq"), None),
-        P(("dp", "side", "seq"), None),
-        P(("dp", "side", "seq"), None),
-        P(("dp", "side", "seq"), None),
-        P(("dp", "side", "seq"), None),
-        P(("dp", "side", "seq"), None),
-        P(("dp", "side", "seq"), None),
-        P(("dp", "side", "seq"), None),
-        P(("dp", "side", "seq"), None),
-        P(("dp", "side", "seq"), None),
-        P(("dp", "side", "seq"), None),
-        P(("dp", "side", "seq"), None),
-        P(("dp", "side", "seq"), None),
-        P(("dp", "side", "seq"), None),
-        P(("dp", "side", "seq"), None),
-        P(("dp", "side", "seq"), None),
-        P(("dp", "side", "seq"), None),
-        P(("dp", "side", "seq"), None),
-        P(("dp", "side", "seq"), None),
-        P(("dp", "side", "seq"), None),
-        P(("dp", "side", "seq"), None),
-        P(("dp", "side", "seq"), None),
-        P(("dp", "side", "seq"), None),
-        P(("dp", "side", "seq"), None),
-        P(("dp", "side", "seq"), None),
-        P(("dp", "side", "seq"), None),
-        P(("dp", "side", "seq"), None),
-        P(("dp", "side", "seq"), None),
-        P(("dp", "side", "seq"), None),
-        P(("dp", "side", "seq"), None),
-        P(("dp", "side", "seq"), None),
-        P(("dp", "side", "seq"), None),
-        P(("dp", "side", "seq"), None),
-        P(("dp", "side", "seq"), None),
-        P(("dp", "side", "seq"), None),
-        P(("dp", "side", "seq"), None),
-        P(("dp", "side", "seq"), None),
-    )
-    out_specs = (
-        P(("dp", "side", "seq"), None),
-        P(("dp", "side", "seq"), None),
-        P(("dp", "side", "seq"), None),
-        P(("dp", "side", "seq"), None),
-        P(),
-        P(("dp", "side", "seq"), None),
-        P(("dp", "side", "seq"), None),
-        P(("dp", "side", "seq"), None),
-        P(("dp", "side", "seq"), None),
-        P(("dp", "side", "seq"), None),
-        P(("dp", "side", "seq"), None),
-        P(("dp", "side", "seq"), None),
-        P(("dp", "side", "seq"), None),
-        P(("dp", "side", "seq"), None),
-        P(("dp", "side", "seq"), None),
-        P(("dp", "side", "seq"), None),
-        P(("dp", "side", "seq"), None),
-        P(("dp", "side", "seq"), None),
-        P(("dp", "side", "seq"), None),
-        P(("dp", "side", "seq"), None),
-        P(("dp", "side", "seq"), None),
-        P(("dp", "side", "seq"), None),
-        P(("dp", "side", "seq"), None),
-        P(("dp", "side", "seq"), None),
-        P(("dp", "side", "seq"), None),
-        P(("dp", "side", "seq"), None),
-        P(("dp", "side", "seq"), None),
-        P(("dp", "side", "seq"), None),
-        P(("dp", "side", "seq"), None),
-        P(("dp", "side", "seq"), None),
-        P(("dp", "side", "seq"), None),
-        P(("dp", "side", "seq"), None),
-        P(("dp", "side", "seq"), None),
-        P(("dp", "side", "seq"), None),
-        P(("dp", "side", "seq"), None),
-        P(("dp", "side", "seq"), None),
-        P(("dp", "side", "seq"), None),
-        P(("dp", "side", "seq"), None),
-        P(("dp", "side", "seq"), None),
-        P(("dp", "side", "seq"), None),
-        P(("dp", "side", "seq"), None),
-    )
+    rows, line = P(AXES, None), P(AXES)
+    in_specs = (rows, rows, line) + (rows,) * 38
+    out_specs = (rows,) * 4 + (P(),) + (rows,) * 36
     return jax.shard_map(body, mesh=mesh, in_specs=in_specs, out_specs=out_specs, check_vma=False)

time: 1470 us -> 294 us (0.20)
  waiting for transfers between devices: 897 us -> 0 us
  Pallas kernels: 117 us -> 292 us
  matrix products: 161 us -> 0 us
  blocking collectives: 150 us -> 0 us
  local copies, waits for them, and re-layouts: 62.6 us -> 1.18 us
  other arithmetic: 39.5 us -> 0 us
  between operations: 23.4 us -> 0.89 us
    reduce_scatter x8 -> x0, waiting for transfers between devices: 874 us -> none  [the longest x1 158 us: body(): lax.psum_scatter(grad_mod, ('dp', 'side', 'seq'), scatter_dimension=0, ti...]
    pallas_call x1 -> x3, Pallas kernels: 117 us -> 292 us  [the longest x1 143 us: backward_all(): pl.pallas_call(lambda *refs: backward_kernel(chunks, count, *refs), out_s...]
    dot_general x108 -> x0, matrix products: 161 us -> none  [the longest x32 59.7 us: matmul(): return jnp.dot(left_side, right_side, preferred_element_type=jnp.float32)]
    all_gather x1 -> x0, blocking collectives: 69.8 us -> none  [body(): lax.all_gather(norm_params.astype(jnp.bfloat16), AXES, axis=0, tiled=True)]
    unnamed x1 -> x0, blocking collectives: 40.3 us -> none
    psum x1 -> x0, blocking collectives: 39.8 us -> none  [body(): grad_norm = jnp.sqrt(lax.psum(local_squares, ('dp', 'side', 'seq')))]
    ppermute x3 -> x0, waiting for transfers between devices: 23.2 us -> none  [shifted(): lax.ppermute(value, axis, [(source, source + steps) for source in range(f...]
    reduce_sum x28 -> x0, other arithmetic: 18.3 us -> none  [the longest x9 13.6 us: body(): local_squares = sum((jnp.sum(gradient * gradient) for gradient in owned))]
  transfers between devices with their start and end apart: 11 -> 0, of which waited for: 8 -> 0; matrix products, arithmetic and copies ran while one was open for 9% -> 0% of each run, Pallas kernels for 0% -> 0%
where the time goes in v2:
time: 294 us
  Pallas kernels  292 us (99%)
    pallas_call x1, Pallas kernels, backward_all(): pl.pallas_call(lambda *refs: backward_kernel(chunks, count, *refs), out_s...  143 us
    pallas_call x1, Pallas kernels, forward_all(): pl.pallas_call(lambda *refs: forward_kernel(chunks, count, *refs), out_sh...  140 us
    pallas_call x1, Pallas kernels, optimizer_all(): pl.pallas_call(optimizer_kernel, out_shape=outs, in_specs=[hbm] * 44 + [v...  9.47 us

profile of v2, /device:TPU:0, one launch (start us, length us, event | category | flops | bytes accessed | tf_op | source)
XLA Modules:
  0.0 293.8 jit_solution(5614047696153506610)
XLA Ops:
  0.7 139.6 %forward.1 = (bf16[768,2304]{1,0:T(8,128)(2,1)}, bf16[768,768]{1,0:T(8,128)(2,1)}, bf16[768,3072]{1,0:T(8,128)(2,1)}, bf16[3072,768]{1,0:T(8,128)(2,1)}, bf16[76...) custom-call(f32[24,2304]{1,0:T(8,128)} %refs_1_.3, ...), custom_call_target="tpu_custom_call" | custom-call | tf_op jit(solution)/shard_map/forward/pallas_call | solution.py:819
  140.3 142.7 %backward.1 = (f32[24,2304]{1,0:T(8,128)}, f32[24,768]{1,0:T(8,128)}, f32[24,3072]{1,0:T(8,128)}, f32[96,768]{1,0:T(8,128)}, f32[24,1024]{1,0:T(8,128)}, /*index...) custom-call(bf16[768,2304]{1,0:T(8,128)(2,1)} %get-tuple-element.122, ...), custom_call_target="tpu_custom_call" | custom-call | tf_op jit(solution)/shard_map/backward/pallas_call | solution.py:1378
  283.0 1.2 slice.3
  284.2 9.5 %optimizer.1 = (f32[24,2304]{1,0:T(8,128)}, f32[24,2304]{1,0:T(8,128)}, f32[24,2304]{1,0:T(8,128)}, f32[24,2304]{1,0:T(8,128)}, f32[24,768]{1,0:T(8,128)}, /*ind...) custom-call(f32[24,2304]{1,0:T(8,128)} %get-tuple-element.149.refs_0, ...), custom_call_target="tpu_custom_call" | custom-call | tf_op jit(solution)/shard_map/optimizer/pallas_call | solution.py:1488

commit v3 on v2

--- a/solution.py
+++ b/solution.py
@@ -57,14 +57,53 @@
     )
 
 
-class Gather:
-    def __init__(self, chunks, masters, fulls, own, slabs, joined, sends, recvs, locs):
-        self.chunks, self.masters, self.fulls = chunks, masters, fulls
-        self.own, self.slabs, self.joined = own, slabs, joined
-        self.sends, self.recvs, self.locs = sends, recvs, locs
+class Line:
+    def __init__(self):
         self.dp, self.side, self.seq, self.near, self.far, self.along, self.before = places()
         self.count = len(self.along) + 1
-        self.started, self.inside = [], {}
+        self.started = {}
+
+    def at(self, dp, side, seq=None):
+        return dp, side, self.seq if seq is None else seq
+
+    def start(self, chunk, copy, go=None):
+        if go is None:
+            copy.start()
+        else:
+            pl.when(go)(copy.start)
+        self.started.setdefault(chunk, []).append((copy, go))
+
+    def sent(self, chunk):
+        for copy, go in self.started.pop(chunk):
+            if go is None:
+                copy.wait_send()
+            else:
+                pl.when(go)(copy.wait_send)
+
+    def goes(self, step):
+        if self.count != 4 or step == 1:
+            return None
+        return self.seq != (3 if step == 0 else 0)
+
+    def inner(self):
+        return jnp.logical_and(self.seq > 0, self.seq < self.count - 1)
+
+    def finish(self):
+        for chunk in list(self.started):
+            self.sent(chunk)
+
+
+class Gather(Line):
+    def __init__(self, chunks, entering, masters, fulls, own, slabs, joined, plain, sems, locs):
+        super().__init__()
+        self.chunks, self.masters, self.fulls = chunks, masters, fulls
+        self.entering = entering
+        self.own, self.slabs, self.joined = own, slabs, joined
+        self.plain, self.sems, self.locs = plain, sems, locs
+        self.inside = {}
+        self.ready = set()
+        self.crossing = [at for at in range(len(chunks)) if at not in plain]
+        self.places = relative(self.dp, self.near, self.far)
 
     def rows(self, group, dp, side):
         size = self.count * self.masters[group].shape[0]
@@ -77,13 +116,20 @@
         group, first, width = self.chunks[chunk]
         return self.fulls[group].at[pl.ds(pl.multiple_of(start, 16), size), pl.ds(first, width)]
 
-    def send(self, chunk, which, source, target, peer):
-        copy = remote(source, target, self.sends.at[chunk, which], self.recvs.at[chunk, which], peer)
-        copy.start()
-        self.started.append(copy)
-
-    def arrived(self, chunk, which, target, peer):
-        remote(target, target, self.sends.at[chunk, which], self.recvs.at[chunk, which], peer).wait_recv()
+    def send(self, chunk, which, source, target, peer, go=None, into=None):
+        into = which if into is None else into
+        copy = remote(source, target, self.sem(0, chunk, which), self.sem(1, chunk, into), peer)
+        self.start(chunk, copy, go)
+
+    def sem(self, kind, chunk, which):
+        if chunk in self.plain:
+            return self.sems[kind].at[self.plain.index(chunk) % RING, which]
+        return self.sems[2 + kind].at[self.crossing.index(chunk), which]
+
+    def arrived(self, chunk, which, target):
+        peer = (self.near, self.side, self.seq)
+        sems = self.sem(0, chunk, which), self.sem(1, chunk, which)
+        remote(target, target, *sems, peer).wait_recv()
 
     def local(self, chunk, source, target):
         copy = pltpu.make_async_copy(source, target, self.locs.at[chunk])
@@ -91,38 +137,64 @@
         self.inside[chunk] = copy
 
     def cast(self, group):
+        if group in self.ready:
+            return
+        self.ready.add(group)
+        self.entering[group].wait()
         rounded = self.masters[group][...].astype(jnp.bfloat16)
         if self.packed(group):
             self.own[group][...] = rounded
         else:
             self.slabs[group][self.seq] = rounded
 
+    def piece(self, chunk, dp, seq):
+        group, start, width = self.chunks[chunk]
+        if not self.packed(group):
+            return self.slabs[group].at[seq, :, pl.ds(start, width)]
+        rows = self.masters[group].shape[0]
+        return self.part(chunk, self.rows(group, dp, self.side)[0] + seq * rows, rows)
+
+    def line(self, chunk, base, source, dp):
+        target = self.piece(chunk, dp, self.seq)
+        for step, peer in enumerate(self.along):
+            self.send(
+                chunk, base + step, source, target, self.at(self.dp, self.side, peer), self.goes(step)
+            )
+
+    def pass_on(self, chunk, base, spare, dp):
+        self.arrived(chunk, base + 1, self.piece(chunk, dp, self.before[1]))
+        if self.count == 4:
+            half = self.seq // 2
+            origin = 3 - 3 * half
+            piece = self.piece(chunk, dp, origin)
+            peer = self.at(self.dp, self.side, 3 - origin)
+            self.send(chunk, spare, piece, piece, peer, self.inner(), base + 2 * half)
+
+    def line_end(self, chunk, base, dp):
+        for step, peer in enumerate(self.before):
+            if step != 1:
+                self.arrived(chunk, base + step, self.piece(chunk, dp, peer))
+
     def first(self, chunk):
         group, start, width = self.chunks[chunk]
-        columns = pl.ds(start, width)
-        rows = self.masters[group].shape[0]
-        base, _ = self.rows(group, self.dp, self.side)
-        for step, peer in enumerate(self.along):
-            if self.packed(group):
-                source = self.own[group].at[:, columns]
-                target = self.part(chunk, base + self.seq * rows, rows)
-            else:
-                source = target = self.slabs[group].at[self.seq, :, columns]
-            self.send(chunk, step, source, target, (self.dp, self.side, peer))
+        at = self.plain.index(chunk)
+        if at >= RING:
+            self.sent(self.plain[at - RING])
+        self.cast(group)
+        target = source = self.piece(chunk, self.dp, self.seq)
         if self.packed(group):
-            self.local(chunk, self.own[group].at[:, columns], self.part(chunk, base + self.seq * rows, rows))
+            source = self.own[group].at[:, pl.ds(start, width)]
+            self.local(chunk, source, target)
+        self.line(chunk, 0, source, self.dp)
+
+    def relay(self, chunk):
+        self.pass_on(chunk, 0, self.count + 7, self.dp)
 
     def second(self, chunk):
         group, start, width = self.chunks[chunk]
         columns = pl.ds(start, width)
-        rows = self.masters[group].shape[0]
         base, size = self.rows(group, self.dp, self.side)
-        for step, peer in enumerate(self.before):
-            if self.packed(group):
-                target = self.part(chunk, base + peer * rows, rows)
-            else:
-                target = self.slabs[group].at[peer, :, columns]
-            self.arrived(chunk, step, target, (self.dp, self.side, peer))
+        self.line_end(chunk, 0, self.dp)
         block = self.part(chunk, base, size)
         if self.packed(group):
             self.inside.pop(chunk).wait()
@@ -140,53 +212,90 @@
             source = joined.at[:, columns]
             self.local(chunk, source, block)
         last = self.count - 1
-        self.send(chunk, last, source, block, (self.near, self.side, self.seq))
-        self.send(chunk, last + 1, source, block, (self.far, self.side, self.seq))
-        self.send(chunk, last + 4, source, block, (self.dp, 1 - self.side, self.seq))
+        self.send(chunk, last, source, block, self.at(self.near, self.side))
+        self.send(chunk, last + 1, source, block, self.at(self.far, self.side))
+        self.send(chunk, last + 4, source, block, self.at(self.dp, 1 - self.side))
 
     def third(self, chunk):
+        last = self.count - 1
+        size = self.rows(self.chunks[chunk][0], self.dp, self.side)[1]
+        self.exchange(chunk, last, last + 1, last + 2, last + 3, 0, size, (last + 5, last + 6))
+
+    def exchange(self, chunk, one, two, three, four, offset, size, sides):
         group = self.chunks[chunk][0]
+        half = size // 2
+        other = self.at(self.dp, 1 - self.side)
+        for place, which, onward, shift, peer, item in (
+            (self.near, one, four, 0, self.far, 0),
+            (self.far, two, three, half, self.near, 1),
+        ):
+            base = self.rows(group, place, self.side)[0] + offset
+            block = self.part(chunk, base, size)
+            self.arrived(chunk, which, block)
+            piece = self.part(chunk, base + shift, half)
+            self.send(chunk, onward, piece, piece, self.at(peer, self.side))
+            if sides:
+                self.send(chunk, sides[item], block, block, other)
+
+    def diagonal(self, chunk, three, four, offset, size):
+        base = self.rows(self.chunks[chunk][0], 3 - self.dp, self.side)[0] + offset
+        half = size // 2
+        self.arrived(chunk, four, self.part(chunk, base, half))
+        self.arrived(chunk, three, self.part(chunk, base + half, half))
+
+    def fourth(self, chunk):
         last = self.count - 1
-        size = self.rows(group, self.dp, self.side)[1]
-        half = size // 2
-        other = (self.dp, 1 - self.side, self.seq)
-        near, far = ((place, self.side, self.seq) for place in (self.near, self.far))
-        base = self.rows(group, self.near, self.side)[0]
+        base, size = self.rows(self.chunks[chunk][0], 3 - self.dp, self.side)
+        self.diagonal(chunk, last + 2, last + 3, 0, size)
         block = self.part(chunk, base, size)
-        self.arrived(chunk, last, block, near)
-        piece = self.part(chunk, base, half)
-        self.send(chunk, last + 3, piece, piece, far)
-        self.send(chunk, last + 5, block, block, other)
-        base = self.rows(group, self.far, self.side)[0]
-        block = self.part(chunk, base, size)
-        self.arrived(chunk, last + 1, block, far)
-        piece = self.part(chunk, base + half, half)
-        self.send(chunk, last + 2, piece, piece, near)
-        self.send(chunk, last + 6, block, block, other)
-
-    def fourth(self, chunk):
-        group = self.chunks[chunk][0]
-        last = self.count - 1
-        base, size = self.rows(group, 3 - self.dp, self.side)
-        half = size // 2
-        self.arrived(chunk, last + 3, self.part(chunk, base, half), (self.far, self.side, self.seq))
-        self.arrived(chunk, last + 2, self.part(chunk, base + half, half), (self.near, self.side, self.seq))
-        block = self.part(chunk, base, size)
-        self.send(chunk, last + 7, block, block, (self.dp, 1 - self.side, self.seq))
-
-    def fifth(self, chunk):
-        group = self.chunks[chunk][0]
-        last = self.count - 1
-        other = (self.dp, 1 - self.side, self.seq)
-        for which, place in enumerate((self.dp, self.near, self.far, 3 - self.dp)):
-            base, size = self.rows(group, place, 1 - self.side)
-            self.arrived(chunk, last + 4 + which, self.part(chunk, base, size), other)
-
-    def finish(self):
-        for copy in self.started:
-            copy.wait_send()
-        for copy in self.inside.values():
-            copy.wait()
+        self.send(chunk, last + 7, block, block, self.at(self.dp, 1 - self.side))
+
+    def fifth(self, chunk, first=None):
+        first = self.count + 3 if first is None else first
+        for which, place in enumerate(self.places):
+            base, size = self.rows(self.chunks[chunk][0], place, 1 - self.side)
+            self.arrived(chunk, first + which, self.part(chunk, base, size))
+
+    def cross(self, chunk, phase):
+        group, start, width = self.chunks[chunk]
+        rows = self.masters[group].shape[0]
+        mine = self.seq * rows
+        hops = self.count - 1
+        spare = 4 + 4 * hops
+        if phase == 0:
+            self.cast(group)
+            source = self.own[group].at[:, pl.ds(start, width)]
+            target = self.piece(chunk, self.dp, self.seq)
+            self.local(chunk, source, target)
+            self.send(chunk, 0, source, target, self.at(self.near, self.side))
+            self.send(chunk, 1, source, target, self.at(self.far, self.side))
+        if phase == 1:
+            self.exchange(chunk, 0, 1, 2, 3, mine, rows, ())
+            self.inside.pop(chunk).wait()
+        if phase == 2:
+            self.diagonal(chunk, 2, 3, mine, rows)
+        for item, place in enumerate(self.places):
+            base = 4 + item * hops
+            if phase == 2 + item:
+                piece = self.piece(chunk, place, self.seq)
+                self.line(chunk, base, piece, place)
+            if phase == 4 + item:
+                self.pass_on(chunk, base, spare + item, place)
+            if phase == 5 + item:
+                self.line_end(chunk, base, place)
+                start, size = self.rows(group, place, self.side)
+                block = self.part(chunk, start, size)
+                self.send(chunk, spare + 4 + item, block, block, self.at(self.dp, 1 - self.side))
+        if phase == CROSS_PHASES - 1:
+            self.fifth(chunk, spare + 4)
+
+
+RING = 6
+CROSS_PHASES = 10
+
+
+def relative(dp, near, far):
+    return (dp, near, far, 3 - dp)
 
 
 def chunk_list(masters):
@@ -200,6 +309,13 @@
             step //= 3
         chunks += [(group, start, step) for start in range(0, width, step)]
     return chunks
+
+
+def cross_chunks(masters, chunks, count):
+    if count != 4 or masters[5][0] % 32 or masters[6][0] % 32:
+        return []
+    inner = [at for at, item in enumerate(chunks) if item[0] == 5]
+    return inner[1:2] + [at for at, item in enumerate(chunks) if item[0] > 5]
 
 
 def shifted(value, axis, steps):
@@ -337,10 +453,6 @@
         self.open = []
 
 
-def relative(dp, near, far):
-    return (dp, near, far, 3 - dp)
-
-
 class LineSum:
     def __init__(self, box, swaps):
         self.box, self.swaps = box, swaps
@@ -383,6 +495,8 @@
 AHEAD_SEQ = 2
 AHEAD_DP = 0
 TASKS = 3
+CROSS_GAP = 5
+NORM_STEP = 1
 
 
 FORWARD_OUT = (
@@ -447,7 +561,7 @@
     return queries, keys, values
 
 
-def forward_kernel(chunks, count, *refs):
+def forward_kernel(chunks, crossing, count, *refs):
     rest = list(refs)
 
     def take(number):
@@ -455,11 +569,13 @@
         del rest[:number]
         return taken
 
-    masters = take(8)
-    tokens, head_in, head_cotangent, ids, norm_rows_own = take(5)
+    given = take(13)
     fulls, sides = take(8), take(8)
     outs = dict(zip([name for name, _, _ in FORWARD_OUT], take(len(FORWARD_OUT))))
     bias_out, norms_out = take(2)
+    held = take(13)
+    masters = held[:8]
+    tokens, head_in, head_cotangent, ids, norm_rows_own = held[8:]
     weights = take(8)
     v = SimpleNamespace(**dict(zip([name for name, _, _ in FORWARD_OUT + FORWARD_LOCAL], take(21))))
     bias, own_row, far_row, box, norms = take(5)
@@ -471,18 +587,28 @@
         else:
             slabs[group] = rest.pop(0)
             joined[group] = rest.pop(0)
-    sends, recvs, locs, loads, moves_sem, swap_send, swap_recv, turn_sem, turn_send, turn_recv = rest
+    entry, *sems, locs, loads, moves_sem, swap_send, swap_recv, turn_sem, turn_send, turn_recv = rest
 
     dp, side, seq, near, far, along, _ = places()
     other = (dp, 1 - side, seq)
+    entering = [
+        pltpu.make_async_copy(source, target, entry.at[item])
+        for item, (source, target) in enumerate(zip(given, held))
+    ]
+    for item in (0, 11, 12, 5, 8, 9, 6, 7, 1, 2, 3, 4, 10):
+        entering[item].start()
     greet(all_peers())
-    flow = Gather(chunks, masters, fulls, own, slabs, joined, sends, recvs, locs)
+    late = [at for at, item in enumerate(chunks) if item[0] == 5 and item[1] >= 2 * HW]
+    plain = [at for at in range(len(chunks)) if at not in crossing + late] + late
+    flow = Gather(chunks, entering, masters, fulls, own, slabs, joined, plain, sems, locs)
     moves = Moves(moves_sem)
     swaps = Swaps(swap_send, swap_recv)
     line = LineSum(box, swaps)
     place = (dp * 2 + side) * count + seq
     width = norm_rows_own.shape[1]
     norms[...] = jnp.zeros(norms.shape, jnp.float32)
+    for item in (11, 12):
+        entering[item].wait()
     norms[0:4, 0:width] = norm_rows_own[...].astype(jnp.bfloat16).astype(jnp.float32)
     spread = pltpu.roll(norms[...], place * width, 1)
     own_row[...] = jnp.broadcast_to(ids[...], own_row.shape).astype(jnp.float32)
@@ -675,9 +801,8 @@
                 grad = head_cotangent[:, columns].astype(jnp.float32) * total
                 v.grad_branch[:, columns] = grad.astype(jnp.bfloat16)
 
-    def stage_mod_end():
+    def stage_shaped():
         put("scale")
-        put("grad_branch")
         share(6, v.shaped, 1)
 
     def stage_inner():
@@ -693,14 +818,23 @@
 
     def stage_outer():
         def emit(columns, total):
-            grown = head_in[:, columns].astype(jnp.float32) + v.gate[:, columns] * total
-            v.head_out[:, columns] = grown.astype(jnp.bfloat16)
+            v.shift[:, columns] = total
             grad = head_cotangent[:, columns].astype(jnp.float32) * total
             v.grad_gate[:, columns] = grad.astype(jnp.bfloat16)
 
         tiles(7, v.lifted, emit)
+        put("grad_gate")
+
+    def stage_gate():
+        put("grad_branch")
+
+        @pl.loop(0, HW // 256)
+        def _(at):
+            columns = span(at, 256)
+            grown = head_in[:, columns].astype(jnp.float32) + v.gate[:, columns] * v.shift[:, columns]
+            v.head_out[:, columns] = grown.astype(jnp.bfloat16)
+
         put("head_out")
-        put("grad_gate")
 
     def chunk_tasks(chunk):
         group, start, width = chunks[chunk]
@@ -724,45 +858,60 @@
             tasks = [stage_cond]
         elif group == 5:
             tasks = [lambda: stage_mod(start, width)]
-            if final:
-                tasks.append(stage_mod_end)
         elif group == 6:
             tasks = [stage_inner]
         else:
             tasks = [stage_outer]
         return [(chunk, task) for task in tasks]
 
-    total = len(chunks)
     line.launch(spread)
     exchange.append(swaps.start(own_row, far_row, other))
-    queue = [item for chunk in range(total) for item in chunk_tasks(chunk)]
-    for step in range(-AHEAD_SEQ, total + 3):
+    queue = [item for at in range(len(chunks)) if at not in late for item in chunk_tasks(at)]
+    place = next(at for at, item in enumerate(queue) if chunks[item[0]][0] == 6)
+    queue.insert(place, (queue[place - 1][0], stage_shaped))
+    queue += [item for at in late for item in chunk_tasks(at)]
+    queue.append((queue[-1][0], stage_gate))
+    total = len(plain)
+    arrived = set()
+    pending = []
+    for step in range(-AHEAD_SEQ, total + 4):
         if step + AHEAD_SEQ < total:
-            group, start, _ = chunks[step + AHEAD_SEQ]
-            if start == 0:
-                flow.cast(group)
-            flow.first(step + AHEAD_SEQ)
+            flow.first(plain[step + AHEAD_SEQ])
+        for item, chunk in enumerate(crossing):
+            phase = step + AHEAD_SEQ - CROSS_GAP * item
+            if 0 <= phase < CROSS_PHASES:
+                flow.cross(chunk, phase)
+                if phase == CROSS_PHASES - 1:
+                    pending.append(chunk)
+        if 0 <= step + AHEAD_DP + 1 < total:
+            flow.relay(plain[step + AHEAD_DP + 1])
         if 0 <= step + AHEAD_DP < total:
-            flow.second(step + AHEAD_DP)
+            flow.second(plain[step + AHEAD_DP])
         if 0 <= step - 1 < total:
-            flow.third(step - 1)
+            flow.third(plain[step - 1])
         if step == -2:
+            for item in (8, 9, 10):
+                entering[item].wait()
             stage_head_norm()
-        if step == -1:
+        if step == NORM_STEP:
             line.launch(line.land())
-        if step == 0:
+        if step == NORM_STEP + 1:
             stage_norm()
         done = 0
-        while queue and queue[0][0] <= step - 3 and (done < TASKS or step >= total):
+        while queue and queue[0][0] in arrived and (done < TASKS or step >= total):
             chunk, task = queue.pop(0)
             if chunk in loading:
                 loading.pop(chunk).wait()
             task()
             done += 1
         if 0 <= step - 2 < total:
-            flow.fourth(step - 2)
-            flow.fifth(step - 2)
-            load(step - 2)
+            flow.fourth(plain[step - 2])
+            flow.fifth(plain[step - 2])
+            pending.append(plain[step - 2])
+        for chunk in pending:
+            load(chunk)
+            arrived.add(chunk)
+        pending = []
     flow.finish()
     moves.finish()
     swaps.finish()
@@ -777,13 +926,16 @@
     count = lax.axis_size("seq")
     chunks = chunk_list([master.shape for master in masters])
     total = len(chunks)
+    crossing = cross_chunks([master.shape for master in masters], chunks, count)
     rows = tokens.shape[0]
     low, full = jnp.bfloat16, jnp.float32
     fulls = [jax.ShapeDtypeStruct((devices * m.shape[0], m.shape[1]), low) for m in masters]
     sides = [jax.ShapeDtypeStruct((devices * m.shape[0] // 2, 2 * rows), low) for m in masters]
     outs = [jax.ShapeDtypeStruct((rows, width), kind) for _, width, kind in FORWARD_OUT]
     extra = [jax.ShapeDtypeStruct((2 * rows, rows), full), jax.ShapeDtypeStruct((8, D), full)]
-    scratch = [pltpu.VMEM(item.shape, low) for item in fulls]
+    given = [*masters, tokens, head_in, head_cotangent, image_ids[None, :], norm_params.T]
+    scratch = [pltpu.VMEM(item.shape, item.dtype) for item in given]
+    scratch += [pltpu.VMEM(item.shape, low) for item in fulls]
     scratch += [pltpu.VMEM((rows, width), kind) for _, width, kind in FORWARD_OUT + FORWARD_LOCAL]
     scratch += [
         pltpu.VMEM((2 * rows, rows), full),
@@ -804,8 +956,11 @@
             scratch.append(pltpu.VMEM((count * depth, width), low))
     dma = pltpu.SemaphoreType.DMA
     scratch += [
-        dma((total, count + 7)),
-        dma((total, count + 7)),
+        dma((13,)),
+        dma((RING, count + 8)),
+        dma((RING, count + 8)),
+        dma((max(1, len(crossing)), 4 * count + 8)),
+        dma((max(1, len(crossing)), 4 * count + 8)),
         dma((total,)),
         dma((total,)),
         dma((16,)),
@@ -815,18 +970,18 @@
         dma((8, 4)),
         dma((8, 4)),
     ]
-    vmem, hbm = pl.BlockSpec(memory_space=pltpu.VMEM), pl.BlockSpec(memory_space=pltpu.HBM)
+    hbm = pl.BlockSpec(memory_space=pltpu.HBM)
     results = pl.pallas_call(
-        lambda *refs: forward_kernel(chunks, count, *refs),
+        lambda *refs: forward_kernel(chunks, crossing, count, *refs),
         out_shape=fulls + sides + outs + extra,
-        in_specs=[vmem] * 13,
+        in_specs=[hbm] * 13,
         out_specs=[hbm] * (16 + len(outs) + 2),
         scratch_shapes=scratch,
         compiler_params=pltpu.CompilerParams(
             collective_id=0, has_side_effects=True, vmem_limit_bytes=63 * 2**20
         ),
         name="forward",
-    )(*masters, tokens, head_in, head_cotangent, image_ids[None, :], norm_params.T)
+    )(*given)
     named = dict(zip([name for name, _, _ in FORWARD_OUT], results[16:]))
     named["bias"], named["norms"] = results[-2:]
     return results[:8], results[8:16], named
@@ -840,13 +995,14 @@
         self.dp, self.side, self.seq, near, far, self.along, _ = places()
         self.near, self.far = (near, self.side, self.seq), (far, self.side, self.seq)
         self.count = len(self.along) + 1
-        self.started = []
+        self.started = {}
         self.coming = {}
 
     def send(self, chunk, which, source, target, peer):
-        copy = remote(source, target, self.sends.at[chunk, which], self.recvs.at[chunk, which], peer)
+        slot = chunk % RING
+        copy = remote(source, target, self.sends.at[slot, which], self.recvs.at[slot, which], peer)
         copy.start()
-        self.started.append(copy)
+        self.started.setdefault(chunk, []).append(copy)
         self.coming[chunk, which] = copy
 
     def land(self, chunk, *which):
@@ -862,6 +1018,7 @@
         group, start, width, size, half = self.shape(chunk)
         columns, part, inbox = pl.ds(start, width), self.parts[group], self.inbox[group]
         upper, lower = pl.ds(0, half), pl.ds(half, half)
+        self.sent(chunk - RING)
         for item, block in enumerate((1, 3)):
             self.send(chunk, item, part.at[block, upper, columns], inbox.at[item, :, columns], self.near)
         for item, block in enumerate((2, 3)):
@@ -935,9 +1092,13 @@
 
         self.tiles(chunk, work)
 
+    def sent(self, chunk):
+        for copy in self.started.pop(chunk, ()):
+            copy.wait_send()
+
     def finish(self):
-        for copy in self.started:
-            copy.wait_send()
+        for chunk in list(self.started):
+            self.sent(chunk)
 
 
 LAG = 1
@@ -978,6 +1139,7 @@
 
     weights, sides = take(8), take(8)
     given = dict(zip(BACKWARD_IN, take(len(BACKWARD_IN))))
+    outs = take(12)
     finals = take(8)
     head_in_grad, tokens_grad, norm_grads, norm_out = take(4)
     grads, parts, inbox, after, slabs, pieces = (take(8) for _ in range(6))
@@ -992,7 +1154,7 @@
     held = [name for name in BACKWARD_IN if name not in into]
     local = SimpleNamespace(**dict(zip(held, take(10))))
     spare, block_grad, attended_grad, back_pair, squares, box, square_box = take(7)
-    sends, recvs, load_sem, side_sem, tile_sem, swap_send, swap_recv = rest
+    sends, recvs, load_sem, side_sem, tile_sem, swap_send, swap_recv, out_sem = rest
 
     dp, side, seq, near, far, along, _ = places()
     other = (dp, 1 - side, seq)
@@ -1000,6 +1162,7 @@
     rows = local.tokens.shape[0]
     own, pair = pl.ds(0, rows), pl.ds(rows, rows)
     swaps = Swaps(swap_send, swap_recv)
+    moves = Moves(out_sem)
     flow = Scatter(chunks, parts, inbox, after, slabs, pieces, finals, squares, sends, recvs)
     loading = {}
     for item, name in enumerate(BACKWARD_IN):
@@ -1037,7 +1200,7 @@
         copy = pltpu.make_async_copy(
             weights[group].at[pl.ds(at * 256, 256), :],
             tile_box.at[item % depth_box, :, pl.ds(0, weights[group].shape[1])],
-            tile_sem.at[item],
+            tile_sem.at[item % depth_box],
         )
         tile_copy[item] = copy
         copy.start()
@@ -1111,6 +1274,9 @@
             flow.third(chunk - LAG - 1)
         if 0 <= chunk - LAG - 2 < total:
             flow.fourth(chunk - LAG - 2)
+            group, start, width = chunks[chunk - LAG - 2]
+            columns = pl.ds(start, width)
+            moves.start(finals[group].at[:, columns], outs[group].at[:, columns])
 
     def stage_outer():
         ready("grad_branch")
@@ -1142,6 +1308,7 @@
             head_in_grad[block, :] = local.head_cotangent[block, :].astype(jnp.float32) + passed
 
         share(5)
+        moves.start(head_in_grad, outs[8])
 
     def stage_mod():
         ready("slope_cond")
@@ -1266,6 +1433,7 @@
             tokens_grad[block, :] = tokens_grad[block, :] + passed
 
         norm_stage(local.tokens, 0, emit)
+        moves.start(tokens_grad, outs[9])
 
     stage_outer()
     stages = [
@@ -1299,6 +1467,7 @@
         elif line.level == 1:
             sums = line.land()
             norm_grads[...] = sums
+            moves.start(norm_grads, outs[10])
     last = LineSum(square_box, swaps)
     last.launch(squares[...])
     last.launch(last.land())
@@ -1307,8 +1476,10 @@
     whole = jnp.sum(flat, axis=1, keepdims=True)
     extra = jnp.sum(jnp.sum(sums * sums, axis=0, keepdims=True), axis=1, keepdims=True)
     norm_out[...] = jnp.broadcast_to(jnp.sqrt(whole + extra), norm_out.shape)
+    moves.start(norm_out, outs[11])
     flow.finish()
     swaps.finish()
+    moves.finish()
 
 
 def backward_chunks(masters):
@@ -1328,7 +1499,7 @@
     total = len(chunks)
     rows = named["tokens"].shape[0]
     low, full = jnp.bfloat16, jnp.float32
-    vmem, hbm = pl.BlockSpec(memory_space=pltpu.VMEM), pl.BlockSpec(memory_space=pltpu.HBM)
+    hbm = pl.BlockSpec(memory_space=pltpu.HBM)
     given = [named[name] for name in BACKWARD_IN]
     outs = [jax.ShapeDtypeStruct(shape, full) for shape in shapes]
     outs += [
@@ -1337,7 +1508,8 @@
         jax.ShapeDtypeStruct((8, D), full),
         jax.ShapeDtypeStruct((8, 128), full),
     ]
-    scratch = [pltpu.VMEM((2 * rows, width), low) for _, width in shapes]
+    scratch = [pltpu.VMEM(item.shape, full) for item in outs]
+    scratch += [pltpu.VMEM((2 * rows, width), low) for _, width in shapes]
     scratch += [pltpu.VMEM((4, count * depth, width), low) for depth, width in shapes]
     scratch += [pltpu.VMEM((4, count * depth // 2, width), low) for depth, width in shapes]
     scratch += [pltpu.VMEM((2, count * depth // 2, width), low) for depth, width in shapes]
@@ -1367,19 +1539,20 @@
     ]
     dma = pltpu.SemaphoreType.DMA
     scratch += [
-        dma((total, 5 + count)),
-        dma((total, 5 + count)),
+        dma((RING, 5 + count)),
+        dma((RING, 5 + count)),
         dma((len(BACKWARD_IN),)),
         dma((8,)),
-        dma((sum(w.shape[0] // 256 for w in weights),)),
+        dma((3,)),
         dma((21 + 2 * count,)),
         dma((21 + 2 * count,)),
+        dma((total + 4,)),
     ]
     return pl.pallas_call(
         lambda *refs: backward_kernel(chunks, count, *refs),
         out_shape=outs,
         in_specs=[hbm] * (16 + len(given)),
-        out_specs=[vmem] * len(outs),
+        out_specs=[hbm] * len(outs),
         scratch_shapes=scratch,
         compiler_params=pltpu.CompilerParams(
             collective_id=1, has_side_effects=True, vmem_limit_bytes=64 * 2**20
@@ -1398,15 +1571,21 @@
 
     given = [take(5) for _ in range(8)]
     passed = take(4)
-    small, grad_norm = take(5), rest.pop(0)
+    small_given = take(6)
     results = [take(4) for _ in range(8)]
     kept = take(4)
-    small_results = take(4)
+    small_outs = take(4)
+    small_held, small_results = take(6), take(4)
+    small, grad_norm = small_held[:5], small_held[5]
     held = [take(5) for _ in range(8)]
     made = [take(4) for _ in range(8)]
     carried = take(4)
-    load_sem, save_sem, pass_sem = rest
-    loads, saves = [], []
+    load_sem, save_sem, pass_sem, small_sem = rest
+    loads, saves, first = [], [], []
+    for item in range(6):
+        copy = pltpu.make_async_copy(small_given[item], small_held[item], small_sem.at[item])
+        copy.start()
+        first.append(copy)
     for group in range(8):
         for item in range(5):
             copy = pltpu.make_async_copy(
@@ -1416,6 +1595,8 @@
             loads.append(copy)
     for item in range(4):
         pltpu.make_async_copy(passed[item], carried[item], pass_sem.at[0, item]).start()
+    for copy in first:
+        copy.wait()
     factor = jnp.minimum(1.0, clip_limit / (grad_norm[0:1, 0:1] + 1e-06))
     keep_old, take_new = average_factors()
 
@@ -1437,6 +1618,12 @@
     turned = pltpu.roll(small[0][...], lax.rem(total - place * width, total), 1)
     own = [turned[0:4, 0:width]] + [ref[...] for ref in small[1:]]
     put(*own, small_results, slice(None), 0.0, learn_rates[8])
+    for item in range(4):
+        copy = pltpu.make_async_copy(
+            small_results[item], small_outs[item], small_sem.at[6 + item]
+        )
+        copy.start()
+        saves.append(copy)
     for group in range(8):
         for item in range(5):
             loads[group * 5 + item].wait()
@@ -1464,7 +1651,7 @@
 
 def optimizer_all(gradients, passed, norm_grads, grad_norm, masters, moments, squares, averages):
     full = jnp.float32
-    vmem, hbm = pl.BlockSpec(memory_space=pltpu.VMEM), pl.BlockSpec(memory_space=pltpu.HBM)
+    hbm = pl.BlockSpec(memory_space=pltpu.HBM)
     given = []
     for group in range(8):
         given += [
@@ -1480,16 +1667,17 @@
     outs = [jax.ShapeDtypeStruct(shape, full) for shape in shapes for _ in range(4)]
     outs += [jax.ShapeDtypeStruct(item.shape, item.dtype) for item in passed]
     outs += [jax.ShapeDtypeStruct(small[0].shape, full) for _ in range(4)]
-    scratch = [pltpu.VMEM(shape, full) for shape in shapes for _ in range(5)]
+    scratch = [pltpu.VMEM(item.shape, full) for item in given[44:] + outs[36:]]
+    scratch += [pltpu.VMEM(shape, full) for shape in shapes for _ in range(5)]
     scratch += [pltpu.VMEM(shape, full) for shape in shapes for _ in range(4)]
     scratch += [pltpu.VMEM(item.shape, item.dtype) for item in passed]
     dma = pltpu.SemaphoreType.DMA
-    scratch += [dma((8, 5)), dma((8, 4)), dma((2, 4))]
+    scratch += [dma((8, 5)), dma((8, 4)), dma((2, 4)), dma((10,))]
     results = pl.pallas_call(
         optimizer_kernel,
         out_shape=outs,
-        in_specs=[hbm] * 44 + [vmem] * 6,
-        out_specs=[hbm] * 36 + [vmem] * 4,
+        in_specs=[hbm] * len(given),
+        out_specs=[hbm] * len(outs),
         scratch_shapes=scratch,
         compiler_params=pltpu.CompilerParams(vmem_limit_bytes=63 * 2**20),
         name="optimizer",
@@ -1502,7 +1690,7 @@
     tokens, head_in, image_ids, out_cotangent, head_cotangent = arrays[:5]
     masters, moments, squares, averages = (arrays[at : at + 9] for at in (5, 14, 23, 32))
     sides = lax.axis_size("dp") == 4 and lax.axis_size("side") == 2
-    if not sides or masters[0].shape[0] % 8 or lax.axis_size("seq") % 2:
+    if not sides or masters[0].shape[0] % 8 or lax.axis_size("seq") != 4:
         return plain_body(*arrays)
     weights, turned, named = forward_all(
         masters[:8], tokens, head_in, head_cotangent, image_ids, masters[8]

time: 294 us -> 277 us (0.942)
  Pallas kernels: 292 us -> 275 us
    pallas_call x2, Pallas kernels: 149 us -> 135 us  [the longest x1 127 us: forward_all(): pl.pallas_call(lambda *refs: forward_kernel(chunks, crossing, count, *ref...]
    pallas_call x1, Pallas kernels: 143 us -> 139 us  [backward_all(): pl.pallas_call(lambda *refs: backward_kernel(chunks, count, *refs), out_s...]
where the time goes in v3:
time: 277 us
  Pallas kernels  275 us (99%)
    pallas_call x1, Pallas kernels, backward_all(): pl.pallas_call(lambda *refs: backward_kernel(chunks, count, *refs), out_s...  139 us
    pallas_call x1, Pallas kernels, forward_all(): pl.pallas_call(lambda *refs: forward_kernel(chunks, crossing, count, *ref...  127 us
    pallas_call x1, Pallas kernels, optimizer_all(): pl.pallas_call(optimizer_kernel, out_shape=outs, in_specs=[hbm] * len(giv...  8.52 us

profile of v3, /device:TPU:0, one launch (start us, length us, event | category | flops | bytes accessed | tf_op | source)
XLA Modules:
  0.0 276.7 jit_solution(14119296395394005633)
XLA Ops:
  0.7 126.9 %forward.1 = (bf16[768,2304]{1,0:T(8,128)(2,1)}, bf16[768,768]{1,0:T(8,128)(2,1)}, bf16[768,3072]{1,0:T(8,128)(2,1)}, bf16[3072,768]{1,0:T(8,128)(2,1)}, bf16[76...) custom-call(f32[24,2304]{1,0:T(8,128)} %refs_1_.3, ...), custom_call_target="tpu_custom_call" | custom-call | tf_op jit(solution)/shard_map/forward/pallas_call | solution.py:974
  127.6 139.2 %backward.1 = (f32[24,2304]{1,0:T(8,128)}, f32[24,768]{1,0:T(8,128)}, f32[24,3072]{1,0:T(8,128)}, f32[96,768]{1,0:T(8,128)}, f32[24,1024]{1,0:T(8,128)}, /*index...) custom-call(bf16[768,2304]{1,0:T(8,128)(2,1)} %get-tuple-element.122, ...), custom_call_target="tpu_custom_call" | custom-call | tf_op jit(solution)/shard_map/backward/pallas_call | solution.py:1551
  266.8 1.2 slice.3
  268.0 8.5 %optimizer.1 = (f32[24,2304]{1,0:T(8,128)}, f32[24,2304]{1,0:T(8,128)}, f32[24,2304]{1,0:T(8,128)}, f32[24,2304]{1,0:T(8,128)}, f32[24,768]{1,0:T(8,128)}, /*ind...) custom-call(f32[24,2304]{1,0:T(8,128)} %get-tuple-element.149.refs_0, ...), custom_call_target="tpu_custom_call" | custom-call | tf_op jit(solution)/shard_map/optimizer/pallas_call | solution.py:1676

commit v4 on v3

--- a/solution.py
+++ b/solution.py
@@ -987,22 +987,26 @@
     return results[:8], results[8:16], named
 
 
-class Scatter:
-    def __init__(self, chunks, parts, inbox, after, slabs, pieces, finals, squares, sends, recvs):
+class Scatter(Line):
+    def __init__(
+        self, chunks, crossing, parts, inbox, after, slabs, pieces, finals, squares, boxes, sems
+    ):
+        super().__init__()
         self.chunks, self.parts, self.inbox, self.after = chunks, parts, inbox, after
         self.slabs, self.pieces, self.finals, self.squares = slabs, pieces, finals, squares
-        self.sends, self.recvs = sends, recvs
-        self.dp, self.side, self.seq, near, far, self.along, _ = places()
-        self.near, self.far = (near, self.side, self.seq), (far, self.side, self.seq)
-        self.count = len(self.along) + 1
-        self.started = {}
+        self.sems, self.boxes, self.crossing = sems, boxes, crossing
+        self.plain = [at for at in range(len(chunks)) if at not in crossing]
+        self.near, self.far = self.at(self.near, self.side), self.at(self.far, self.side)
         self.coming = {}
 
-    def send(self, chunk, which, source, target, peer):
-        slot = chunk % RING
-        copy = remote(source, target, self.sends.at[slot, which], self.recvs.at[slot, which], peer)
-        copy.start()
-        self.started.setdefault(chunk, []).append(copy)
+    def send(self, chunk, which, source, target, peer, go=None):
+        if chunk in self.crossing:
+            kind, slot = 2, self.crossing.index(chunk)
+        else:
+            kind, slot = 0, self.plain.index(chunk) % RING
+        sems = self.sems[kind].at[slot, which], self.sems[kind + 1].at[slot, which]
+        copy = remote(source, target, *sems, peer)
+        self.start(chunk, copy, go)
         self.coming[chunk, which] = copy
 
     def land(self, chunk, *which):
@@ -1018,7 +1022,9 @@
         group, start, width, size, half = self.shape(chunk)
         columns, part, inbox = pl.ds(start, width), self.parts[group], self.inbox[group]
         upper, lower = pl.ds(0, half), pl.ds(half, half)
-        self.sent(chunk - RING)
+        at = self.plain.index(chunk)
+        if at >= RING:
+            self.sent(self.plain[at - RING])
         for item, block in enumerate((1, 3)):
             self.send(chunk, item, part.at[block, upper, columns], inbox.at[item, :, columns], self.near)
         for item, block in enumerate((2, 3)):
@@ -1092,16 +1098,118 @@
 
         self.tiles(chunk, work)
 
-    def sent(self, chunk):
-        for copy in self.started.pop(chunk, ()):
-            copy.wait_send()
-
-    def finish(self):
-        for chunk in list(self.started):
-            self.sent(chunk)
-
-
+    def cross(self, chunk, phase):
+        group, start, width, size, _ = self.shape(chunk)
+        columns, part = pl.ds(start, width), self.parts[group]
+        depth = size // self.count
+        half = depth // 2
+        box, got, sums, inbox, after = self.boxes[self.crossing.index(chunk)]
+        final = self.finals[group]
+
+        def rows(seq):
+            return pl.ds(pl.multiple_of(seq * depth, 16), depth)
+
+        def tiles(work):
+            @pl.loop(0, width // 256)
+            def _(at):
+                at = pl.multiple_of(at * 256, 256)
+                work(pl.ds(at, 256), pl.ds(pl.multiple_of(start + at, 256), 256))
+
+        def pair_peer(step):
+            return self.at(self.dp, self.side, self.along[step])
+
+        if phase < 4:
+            for step in (0, 2):
+                self.send(
+                    chunk,
+                    4 * phase + step,
+                    part.at[phase, rows(self.along[step]), columns],
+                    got.at[phase, step],
+                    pair_peer(step),
+                    self.goes(step),
+                )
+            beside = self.seq + 1 - 2 * lax.rem(self.seq, 2)
+            self.send(
+                chunk,
+                4 * phase + 3,
+                part.at[phase, rows(3 - self.seq), columns],
+                box.at[phase],
+                self.at(self.dp, self.side, beside),
+                jnp.logical_not(self.inner()),
+            )
+        if 2 <= phase < 6:
+            block = phase - 2
+
+            @pl.when(self.inner())
+            def _():
+                self.coming[chunk, 4 * block + 3].wait_recv()
+
+                def work(here, there):
+                    total = part[block, rows(self.along[1]), there].astype(jnp.float32)
+                    total = total + box[block, :, here].astype(jnp.float32)
+                    part[block, rows(self.along[1]), there] = total.astype(jnp.bfloat16)
+
+                tiles(work)
+
+            self.send(
+                chunk,
+                4 * block + 1,
+                part.at[block, rows(self.along[1]), columns],
+                got.at[block, 1],
+                pair_peer(1),
+            )
+        if 4 <= phase < 8:
+            block = phase - 4
+            self.land(chunk, 4 * block + 1)
+            pl.when(self.seq != 0)(self.coming[chunk, 4 * block].wait_recv)
+            pl.when(self.seq != 3)(self.coming[chunk, 4 * block + 2].wait_recv)
+
+            def work(here, there):
+                total = part[block, rows(self.seq), there].astype(jnp.float32)
+                for step in range(3):
+                    total = total + got[block, step, :, here].astype(jnp.float32)
+                sums[block, :, here] = total.astype(jnp.bfloat16)
+
+            tiles(work)
+        upper, lower = pl.ds(0, half), pl.ds(half, half)
+        if phase == 7:
+            for item, block in enumerate((1, 3)):
+                self.send(chunk, 16 + item, sums.at[block, upper, :], inbox.at[item], self.near)
+            for item, block in enumerate((2, 3)):
+                self.send(chunk, 18 + item, sums.at[block, lower, :], inbox.at[2 + item], self.far)
+        if phase == 8:
+            self.land(chunk, 16, 17, 18, 19)
+
+            def work(here, there):
+                for block, part_rows, item in ((2, upper, 1), (1, lower, 3)):
+                    total = sums[block, part_rows, here].astype(jnp.float32)
+                    total = total + inbox[item, :, here].astype(jnp.float32)
+                    sums[block, part_rows, here] = total.astype(jnp.bfloat16)
+
+            tiles(work)
+            self.send(chunk, 20, sums.at[1, lower, :], after.at[0], self.near)
+            self.send(chunk, 21, sums.at[2, upper, :], after.at[1], self.far)
+        if phase == 9:
+            self.land(chunk, 20, 21)
+
+            def work(here, there):
+                for part_rows, item, last in ((upper, 0, 1), (lower, 2, 0)):
+                    total = sums[0, part_rows, here].astype(jnp.float32)
+                    total = total + inbox[item, :, here].astype(jnp.float32)
+                    total = total + after[last, :, here].astype(jnp.float32)
+                    final[part_rows, there] = total
+                    self.squares[0:1, :] += jnp.sum(total * total, axis=0, keepdims=True)
+
+            tiles(work)
+
+
+CROSS_STEPS = (1,)
+CROSS_LAST = 10
 LAG = 1
+MID = 1
+LATE = 3
+NCROSS = 1
+EXTRA = (0,)
 
 
 BACKWARD_IN = (
@@ -1129,7 +1237,7 @@
     return scale * (grads - first - values * second)
 
 
-def backward_kernel(chunks, count, *refs):
+def backward_kernel(chunks, crossing, count, *refs):
     rest = list(refs)
 
     def take(number):
@@ -1153,17 +1261,29 @@
     }
     held = [name for name in BACKWARD_IN if name not in into]
     local = SimpleNamespace(**dict(zip(held, take(10))))
-    spare, block_grad, attended_grad, back_pair, squares, box, square_box = take(7)
-    sends, recvs, load_sem, side_sem, tile_sem, swap_send, swap_recv, out_sem = rest
+    spare, attended_grad, back_pair, squares, box, square_box = take(6)
+    boxes = [take(5) for _ in crossing]
+    *sems, load_sem, side_sem, tile_sem, swap_send, swap_recv, out_sem = rest
 
     dp, side, seq, near, far, along, _ = places()
     other = (dp, 1 - side, seq)
+    for _, got, _, _, _ in boxes:
+        @pl.when(seq == 0)
+        def _():
+            got[:, 0] = jnp.zeros(got.shape[:1] + got.shape[2:], got.dtype)
+
+        @pl.when(seq == count - 1)
+        def _():
+            got[:, 2] = jnp.zeros(got.shape[:1] + got.shape[2:], got.dtype)
+
     greet(all_peers())
     rows = local.tokens.shape[0]
     own, pair = pl.ds(0, rows), pl.ds(rows, rows)
     swaps = Swaps(swap_send, swap_recv)
     moves = Moves(out_sem)
-    flow = Scatter(chunks, parts, inbox, after, slabs, pieces, finals, squares, sends, recvs)
+    flow = Scatter(
+        chunks, crossing, parts, inbox, after, slabs, pieces, finals, squares, boxes, sems
+    )
     loading = {}
     for item, name in enumerate(BACKWARD_IN):
         target = into[name] if name in into else getattr(local, name)
@@ -1263,24 +1383,35 @@
             if group in slim and slim.index(group) + 2 < len(slim):
                 side_load(slim[slim.index(group) + 2])
 
-    def step(chunk):
-        total = len(chunks)
-        if chunk < total:
-            product(chunk)
-            flow.first(chunk)
-        if 0 <= chunk - LAG < total:
-            flow.second(chunk - LAG)
-        if 0 <= chunk - LAG - 1 < total:
-            flow.third(chunk - LAG - 1)
-        if 0 <= chunk - LAG - 2 < total:
-            flow.fourth(chunk - LAG - 2)
-            group, start, width = chunks[chunk - LAG - 2]
-            columns = pl.ds(start, width)
-            moves.start(finals[group].at[:, columns], outs[group].at[:, columns])
+    plain = flow.plain
+
+    def done(chunk):
+        group, start, width = chunks[chunk]
+        columns = pl.ds(start, width)
+        moves.start(finals[group].at[:, columns], outs[group].at[:, columns])
+
+    def step(at):
+        total = len(plain)
+        if at < total:
+            product(plain[at])
+            flow.first(plain[at])
+            earlier = plain[at - 1] if at else -1
+            for chunk in range(earlier + 1, plain[at]):
+                product(chunk)
+        for chunk, begin in zip(crossing, CROSS_STEPS):
+            if 0 <= at - begin < CROSS_LAST:
+                flow.cross(chunk, at - begin)
+                if at - begin == CROSS_LAST - 1:
+                    done(chunk)
+        if 0 <= at - LAG < total:
+            flow.second(plain[at - LAG])
+        if 0 <= at - LAG - MID < total:
+            flow.third(plain[at - LAG - MID])
+        if 0 <= at - LAG - LATE < total:
+            flow.fourth(plain[at - LAG - LATE])
+            done(plain[at - LAG - LATE])
 
     def stage_outer():
-        ready("grad_branch")
-        share(7)
         ready("slope_middle")
 
         def emit(columns, total):
@@ -1325,7 +1456,7 @@
 
         def emit(columns, total):
             grad = local.out_cotangent[:, columns].astype(jnp.float32) + total
-            block_grad[:, columns] = grad
+            tokens_grad[:, columns] = grad
             grads[3][own, columns] = grad.astype(jnp.bfloat16)
 
         back(4, emit)
@@ -1361,7 +1492,7 @@
         ready("hidden", "norms")
 
         def emit(block, passed):
-            grad = block_grad[block, :] + passed
+            grad = tokens_grad[block, :] + passed
             tokens_grad[block, :] = grad
             grads[1][block, :] = grad.astype(jnp.bfloat16)
 
@@ -1435,8 +1566,10 @@
         norm_stage(local.tokens, 0, emit)
         moves.start(tokens_grad, outs[9])
 
-    stage_outer()
+    ready("grad_branch")
+    share(7)
     stages = [
+        stage_outer,
         stage_inner,
         stage_mod,
         stage_cond,
@@ -1451,15 +1584,17 @@
         stage_attend,
     ]
     line = LineSum(box, swaps)
-    total = len(chunks)
-    for chunk in range(total + LAG + 3):
-        group = chunks[min(chunk, total - 1)][0]
-        needed = {7: 0, 6: 0, 5: 1, 4: 2, 3: 3, 2: 4, 1: 5, 0: 11}[group]
-        while stages and 12 - len(stages) < needed:
+    total = len(plain)
+    for chunk in range(max(total + LAG + LATE, CROSS_STEPS[-1] + CROSS_LAST)):
+        group = chunks[plain[min(chunk, total - 1)]][0]
+        needed = {7: 0, 6: 1, 5: 2, 4: 3, 3: 4, 2: 5, 1: 6, 0: 12}[group]
+        while stages and 13 - len(stages) < needed:
             stages.pop(0)()
         step(chunk)
         if stages:
             stages.pop(0)()
+            if chunk in EXTRA:
+                stages.pop(0)()
             if not stages:
                 line.launch(norm_grads[...])
         elif line.level == 0:
@@ -1496,7 +1631,9 @@
     count = lax.axis_size("seq")
     shapes = [master.shape for master in masters]
     chunks = backward_chunks(shapes)
-    total = len(chunks)
+    inner = [at for at, item in enumerate(chunks) if item[0] == 5]
+    crossing = [at for at, item in enumerate(chunks) if item[0] == 6][:1] + inner[1::2]
+    crossing = crossing[:NCROSS]
     rows = named["tokens"].shape[0]
     low, full = jnp.bfloat16, jnp.float32
     hbm = pl.BlockSpec(memory_space=pltpu.HBM)
@@ -1511,10 +1648,12 @@
     scratch = [pltpu.VMEM(item.shape, full) for item in outs]
     scratch += [pltpu.VMEM((2 * rows, width), low) for _, width in shapes]
     scratch += [pltpu.VMEM((4, count * depth, width), low) for depth, width in shapes]
-    scratch += [pltpu.VMEM((4, count * depth // 2, width), low) for depth, width in shapes]
-    scratch += [pltpu.VMEM((2, count * depth // 2, width), low) for depth, width in shapes]
-    scratch += [pltpu.VMEM((count, depth, width), low) for depth, width in shapes]
-    scratch += [pltpu.VMEM((count - 1, depth, width), low) for depth, width in shapes]
+    used = {item[0] for at, item in enumerate(chunks) if at not in crossing}
+    boxed = [shape if at in used else (16, 128) for at, shape in enumerate(shapes)]
+    scratch += [pltpu.VMEM((4, count * depth // 2, width), low) for depth, width in boxed]
+    scratch += [pltpu.VMEM((2, count * depth // 2, width), low) for depth, width in boxed]
+    scratch += [pltpu.VMEM((count, depth, width), low) for depth, width in boxed]
+    scratch += [pltpu.VMEM((count - 1, depth, width), low) for depth, width in boxed]
     scratch += [
         pltpu.VMEM((2, HW // 2, 2 * rows), low),
         pltpu.VMEM((2 * D, 2 * rows), low),
@@ -1530,26 +1669,37 @@
         pltpu.VMEM((2 * rows, rows), full),
         pltpu.VMEM((rows, D), low),
         pltpu.VMEM((rows, 2 * D), full),
-        pltpu.VMEM((rows, D), full),
         pltpu.VMEM((rows, D), low),
         pltpu.VMEM((rows, 2 * D), low),
         pltpu.VMEM((8, 256), full),
         pltpu.VMEM((count + 8, 8, D), full),
         pltpu.VMEM((count + 8, 8, 256), full),
     ]
+    for chunk in crossing:
+        group, _, width = chunks[chunk]
+        depth = shapes[group][0]
+        scratch += [
+            pltpu.VMEM((4, depth, width), low),
+            pltpu.VMEM((4, count - 1, depth, width), low),
+            pltpu.VMEM((4, depth, width), low),
+            pltpu.VMEM((4, depth // 2, width), low),
+            pltpu.VMEM((2, depth // 2, width), low),
+        ]
     dma = pltpu.SemaphoreType.DMA
     scratch += [
         dma((RING, 5 + count)),
         dma((RING, 5 + count)),
+        dma((max(1, len(crossing)), 22)),
+        dma((max(1, len(crossing)), 22)),
         dma((len(BACKWARD_IN),)),
         dma((8,)),
         dma((3,)),
         dma((21 + 2 * count,)),
         dma((21 + 2 * count,)),
-        dma((total + 4,)),
+        dma((len(chunks) + 4,)),
     ]
     return pl.pallas_call(
-        lambda *refs: backward_kernel(chunks, count, *refs),
+        lambda *refs: backward_kernel(chunks, crossing, count, *refs),
         out_shape=outs,
         in_specs=[hbm] * (16 + len(given)),
         out_specs=[hbm] * len(outs),

time: 277 us -> 274 us (0.989)
  Pallas kernels: 275 us -> 272 us
    pallas_call x1, Pallas kernels: 139 us -> 136 us  [backward_all(): pl.pallas_call(lambda *refs: backward_kernel(chunks, crossing, count, *re...]
where the time goes in v4:
time: 274 us
  Pallas kernels  272 us (99%)
    pallas_call x1, Pallas kernels, backward_all(): pl.pallas_call(lambda *refs: backward_kernel(chunks, crossing, count, *re...  136 us
    pallas_call x1, Pallas kernels, forward_all(): pl.pallas_call(lambda *refs: forward_kernel(chunks, crossing, count, *ref...  127 us
    pallas_call x1, Pallas kernels, optimizer_all(): pl.pallas_call(optimizer_kernel, out_shape=outs, in_specs=[hbm] * len(giv...  8.52 us

profile of v4, /device:TPU:0, one launch (start us, length us, event | category | flops | bytes accessed | tf_op | source)
XLA Modules:
  0.0 273.8 jit_solution(5820061028592931378)
XLA Ops:
  0.7 126.9 %forward.1 = (bf16[768,2304]{1,0:T(8,128)(2,1)}, bf16[768,768]{1,0:T(8,128)(2,1)}, bf16[768,3072]{1,0:T(8,128)(2,1)}, bf16[3072,768]{1,0:T(8,128)(2,1)}, bf16[76...) custom-call(f32[24,2304]{1,0:T(8,128)} %refs_1_.3, ...), custom_call_target="tpu_custom_call" | custom-call | tf_op jit(solution)/shard_map/forward/pallas_call | solution.py:974
  127.6 136.3 %backward.1 = (f32[24,2304]{1,0:T(8,128)}, f32[24,768]{1,0:T(8,128)}, f32[24,3072]{1,0:T(8,128)}, f32[96,768]{1,0:T(8,128)}, f32[24,1024]{1,0:T(8,128)}, /*index...) custom-call(bf16[768,2304]{1,0:T(8,128)(2,1)} %get-tuple-element.122, ...), custom_call_target="tpu_custom_call" | custom-call | tf_op jit(solution)/shard_map/backward/pallas_call | solution.py:1701
  263.9 1.2 slice.3
  265.1 8.5 %optimizer.1 = (f32[24,2304]{1,0:T(8,128)}, f32[24,2304]{1,0:T(8,128)}, f32[24,2304]{1,0:T(8,128)}, f32[24,2304]{1,0:T(8,128)}, f32[24,768]{1,0:T(8,128)}, /*ind...) custom-call(f32[24,2304]{1,0:T(8,128)} %get-tuple-element.149.refs_0, ...), custom_call_target="tpu_custom_call" | custom-call | tf_op jit(solution)/shard_map/optimizer/pallas_call | solution.py:1826
